TPU v7x, 512 devices: a whole 4x8x8 slice. The times are simulated.
512 devices in a mesh: brick: 128 (over y, z, core), ch: 4 (over x).
Axes of the slice: x: 4, y: 8, z: 8, core: 2. Of those that a mesh axis runs over, the one named last changes fastest.
Arguments:
- features: bfloat16 [256, 16384], P('ch', 'brick'), may hold values from -6 to 6
- owner_map: int32 [16384, 1], P('brick'), may hold values from 0 to 127; in each aligned block of 128 rows (0 to 127, 128 to 255, ...) at most 2 rows name the same one
- kernel_map: int32 [27, 32768], P(None, 'brick'), may hold values from 0 to 320, as said below
- send_lists: int32 [2, 4096], P(None, 'brick'), may hold values from 0 to 255
- drop_first: int32 [256, 32768], P('ch', 'brick'), may hold values 0 or 1
- drop_second: int32 [256, 32768], P('ch', 'brick'), may hold values 0 or 1
- weight_first: bfloat16 [27, 256, 256], P(None, 'ch'), may hold values from -0.15625 to 0.15625
- weight_second: bfloat16 [27, 256, 256], P(None, 'ch'), may hold values from -0.15625 to 0.15625
- cotangent: bfloat16 [256, 32768], P('ch', 'brick'), may hold values from -24 to 24
Outputs:
- block_out: bfloat16 [256, 32768], P('ch', 'brick')
- grad_features: bfloat16 [256, 16384], P('ch', 'brick')
- grad_weight_first: bfloat16 [27, 256, 256], P(None, 'ch')
- grad_weight_second: bfloat16 [27, 256, 256], P(None, 'ch')
Inputs may be any that keep to these rules, and one draw needn't show every extreme that they name: `owner_map`: among the rows of one scan group, at most 2 are owned by the same brick. `kernel_map`: column 320 means that the neighbour is absent; in the middle offset row, slot i of every brick names column 32 + i.
All inputs are finite; a program needn't handle non-finite values. No bound on the sum of `drop_first` or of `drop_second` on one device may be relied on, other than what follows from the above.
Results may differ from a plain program's by a relative error of at most 0.0064.
Values may be sent and summed in bfloat16 or wider, within the bound.
A program may use at most 64 MiB of HBM per device.

v0:
```python
import jax
import jax.numpy as jnp
from jax import lax
from jax.sharding import PartitionSpec as P

KEEP_RATE = 0.9


def with_halo(block, sides, width):
    for axis, dim in sides:
        count = lax.axis_size(axis)
        forward = [(i, i + 1) for i in range(count - 1)]
        backward = [(target, source) for source, target in forward]
        low = lax.ppermute(
            lax.slice_in_dim(block, block.shape[dim] - width, None, axis=dim), axis, forward
        )
        high = lax.ppermute(lax.slice_in_dim(block, 0, width, axis=dim), axis, backward)
        block = jnp.concatenate([low, block, high], axis=dim)
    return block


def slope_silu(value):
    sig = jax.nn.sigmoid(value)
    return sig * (1.0 + value * (1.0 - sig))


def spread(field, send_lists):
    rim_width = send_lists.shape[1]
    outgoing = jnp.concatenate(
        [jnp.take(field, send_lists[0], axis=1), jnp.take(field, send_lists[1], axis=1)], axis=1
    )
    padded = with_halo(outgoing, (("brick", 1),), rim_width)
    return jnp.concatenate([padded[:, :rim_width], field, padded[:, 3 * rim_width :]], axis=1)


def convolve(extended, kernel_map, weight):
    gathered = jnp.take(extended, kernel_map, axis=1, mode="fill", fill_value=0)
    return (
        lax.psum_scatter(
            jnp.einsum("ckr,kco->or", gathered, weight, preferred_element_type=jnp.float32),
            "ch",
            scatter_dimension=0,
            tiled=True,
        ),
        gathered,
    )


def adjoint(gathered, kernel_map, grad_local, weight, extent):
    gathered_grad = lax.all_gather(grad_local, "ch", axis=0, tiled=True)
    weight_grad = jnp.einsum(
        "ckr,or->kco", gathered, gathered_grad, preferred_element_type=jnp.float32
    )
    pushed = jnp.einsum("kco,or->ckr", weight, gathered_grad, preferred_element_type=jnp.float32)
    returned = (
        jnp.zeros((pushed.shape[0], extent), jnp.float32).at[:, kernel_map].add(pushed, mode="drop")
    )
    return (weight_grad, returned)


def fold_back(returned, send_lists, slot_count):
    rim_width = send_lists.shape[1]
    borders = jnp.concatenate(
        [returned[:, :rim_width], returned[:, rim_width + slot_count :]], axis=1
    )
    padded = with_halo(borders, (("brick", 1),), rim_width)
    interior = returned[:, rim_width : rim_width + slot_count]
    interior = interior.at[:, send_lists[0]].add(padded[:, :rim_width])
    return interior.at[:, send_lists[1]].add(padded[:, 3 * rim_width :])


def local(
    features,
    owner_map,
    kernel_map,
    send_lists,
    drop_first,
    drop_second,
    weight_first,
    weight_second,
    cotangent,
):
    bricks = lax.axis_size("brick")
    channels = features.shape[0]
    slot_count = 2 * features.shape[1]
    capacity = slot_count // bricks
    targets = owner_map[:, 0]
    matches = (targets[:, None] == jnp.arange(bricks, dtype=jnp.int32)[None, :]).astype(jnp.int32)
    running = jnp.cumsum(matches, axis=0)
    ordinal = jnp.sum((running - 1) * matches, axis=1)
    columns = targets * capacity + ordinal
    outgoing = jnp.zeros((channels, slot_count), features.dtype).at[:, columns].set(features)
    tallies = jnp.sum(matches, axis=0)[None, :].astype(jnp.bfloat16)
    arrived, arrived_tallies = (
        lax.all_to_all(
            outgoing.reshape(channels, bricks, capacity),
            "brick",
            split_axis=1,
            concat_axis=1,
            tiled=True,
        ),
        lax.all_to_all(tallies, "brick", split_axis=1, concat_axis=1, tiled=True),
    )
    voxels = arrived.reshape(channels, slot_count)
    occupied = (
        jnp.arange(capacity, dtype=jnp.int32)[None, :]
        < arrived_tallies[0].astype(jnp.int32)[:, None]
    )
    occupied = occupied.reshape(slot_count).astype(jnp.float32)
    keep_first = occupied[None, :] * drop_first.astype(jnp.float32) / KEEP_RATE
    keep_second = occupied[None, :] * drop_second.astype(jnp.float32) / KEEP_RATE
    extended_voxels = spread(voxels, send_lists)
    extent = extended_voxels.shape[1]
    conv_first, gathered_voxels = convolve(extended_voxels, kernel_map, weight_first)
    hidden = (jax.nn.silu(conv_first) * keep_first).astype(jnp.bfloat16)
    extended_hidden = spread(hidden, send_lists)
    conv_second, gathered_hidden = convolve(extended_hidden, kernel_map, weight_second)
    summed = voxels.astype(jnp.float32) + keep_second * conv_second
    block_out = jax.nn.silu(summed).astype(jnp.bfloat16)
    grad_pre = cotangent.astype(jnp.float32) * slope_silu(summed)
    grad_second = (grad_pre * keep_second).astype(jnp.bfloat16)
    weight_grad_second, returned_second = adjoint(
        gathered_hidden, kernel_map, grad_second, weight_second, extent
    )
    grad_hidden = fold_back(returned_second, send_lists, slot_count)
    grad_first = (grad_hidden * keep_first * slope_silu(conv_first)).astype(jnp.bfloat16)
    weight_grad_first, returned_first = adjoint(
        gathered_voxels, kernel_map, grad_first, weight_first, extent
    )
    weight_grad_first, weight_grad_second = lax.psum(
        (weight_grad_first, weight_grad_second), "brick"
    )
    grad_voxels = (grad_pre + fold_back(returned_first, send_lists, slot_count)).astype(
        jnp.bfloat16
    )
    homeward = lax.all_to_all(
        grad_voxels.reshape(channels, bricks, capacity),
        "brick",
        split_axis=1,
        concat_axis=1,
        tiled=True,
    )
    grad_features = jnp.take(homeward.reshape(channels, slot_count), columns, axis=1)
    factor = float(bricks * slot_count) ** (-0.5)
    return (
        block_out,
        grad_features,
        (weight_grad_first * factor).astype(jnp.bfloat16),
        (weight_grad_second * factor).astype(jnp.bfloat16),
    )


def solution(mesh):
    return jax.shard_map(
        local,
        mesh=mesh,
        in_specs=(
            P("ch", "brick"),
            P("brick", None),
            P(None, "brick"),
            P(None, "brick"),
            P("ch", "brick"),
            P("ch", "brick"),
            P(None, "ch", None),
            P(None, "ch", None),
            P("ch", "brick"),
        ),
        out_specs=(P("ch", "brick"), P("ch", "brick"), P(None, "ch", None), P(None, "ch", None)),
        check_vma=False,
    )
```

profile of v0, /device:TPU:1, one launch (start us, length us, event | category | flops | bytes accessed | tf_op | source)
XLA Modules:
  0.0 439.1 jit_solution(2850545359836102251)
XLA Ops:
  13.1 18.4 %all-to-all-start = ((bf16[64,128,2]{0,2,1:T(2,128)(2,1)}), bf16[64,128,2]{0,2,1:T(2,128)(2,1)S(1)}, u32[]{:S(2)}, u32[]{:S(2)}) async-start(bf16[64,128,2]{0,2,1:T(2,128)(2,1)} %bitcast.4), calls=%async_computation | async-start | bytes 131072 | tf_op jit(solution)/shard_map/all_to_all | solution.py:95
  34.0 9.0 %all-to-all-done = bf16[64,128,2]{0,2,1:T(2,128)(2,1)S(1)} async-done(((bf16[64,128,2]{0,2,1:T(2,128)(2,1)}), bf16[64,128,2]{0,2,1:T(2,128)(2,1)S(1)}, u32[]{:S(2)}, u32[]{:S(2)}) %all-to-all-start) | async-done | bytes 32800 | tf_op jit(solution)/shard_map/all_to_all | solution.py:95
  43.7 2.9 collective-permute-start
  49.2 3.0 collective-permute-done.1
  52.3 13.0 %gather_fusion.3 = bf16[6912,64]{1,0:T(8,128)(2,1)S(1)} fusion(bf16[64,320]{0,1:T(8,128)(2,1)S(1)} %pad_maximum_fusion, s32[7168]{0:T(1024)S(1)} %pad_clamp_fusion), kind=kCustom, calls=%fused_computation.1.clone | custom fusion | bytes 1797120 | tf_op jit(solution)/shard_map/jit(_take)/gather | solution.py:37
  69.4 20.6 %all_to_all.16 = bf16[1,128,1]{2,0,1:T(2,128)(2,1)S(1)} all-to-all(bf16[1,128,1]{2,0,1:T(2,128)(2,1)S(1)} %copy.100), channel_id=1, replica_groups=mesh['brick'=128,'ch'=4] {'brick'}, dimensions={1} | all-to-all | bytes 512 | tf_op jit(solution)/shard_map/all_to_all | solution.py:102
  90.0 2.4 convert_reduce_fusion
  95.0 2.9 collective-permute-start.2
  100.0 3.1 collective-permute-done.3
  103.4 13.0 %gather_fusion.6 = bf16[6912,64]{1,0:T(8,128)(2,1)S(1)} fusion(bf16[64,320]{0,1:T(8,128)(2,1)S(1)} %copy.108, s32[7168]{0:T(1024)S(1)} %copy-done.7), kind=kCustom, calls=%fused_computation.5.clone | custom fusion | bytes 1797120 | tf_op jit(solution)/shard_map/jit(_take)/gather | solution.py:37
  119.4 22.5 %reduce-scatter.9.cloned.1.call-done = f32[64,256]{1,0:T(8,128)} async-done(((f32[256,256]{1,0:T(8,128)}), f32[64,256]{1,0:T(8,128)}) %reduce-scatter.9.cloned.1.call-update) | async-done | bytes 65552 | tf_op jit(solution)/shard_map/reduce_scatter | solution.py:39
  142.8 9.3 %all_gather.6 = bf16[256,256]{1,0:T(8,128)(2,1)S(1)} all-gather(bf16[64,256]{1,0:T(8,128)(2,1)S(1)} %multiply_convert_fusion.3), channel_id=1, replica_groups=mesh['brick'=128,'ch'=4] {'ch'}, dimensions={0}, use_global_device_ids=true | all-gather | bytes 163840 | tf_op jit(solution)/shard_map/all_gather | solution.py:50
  153.1 2.5 copy.120
  155.6 39.1 %scatter_custom_fusion.1 = f32[64,320]{0,1:T(8,128)S(1)} fusion(s32[6912]{0:T(1024)} %copy-done.18, f32[6912,64]{1,0:T(8,128)} %bitcast.101, f32[]{:T(128)} %constant.44.clone.1), kind=kCustom, calls=%fused_computation.40 | custom fusion | flops 442368 | bytes 82432 | tf_op jit(solution)/shard_map/scatter-add | solution.py:56
  194.7 8.9 %collective-permute-start.4 = (f32[64,32]{0,1:T(8,128)S(1)}, f32[64,32]{0,1:T(8,128)S(1)}, u32[]{:S(2)}, u32[]{:S(2)}) collective-permute-start(f32[64,32]{0,1:T(8,128)S(1)} %get-tuple-element.45), channel_id=1, source_target_pairs={{0,4},{4,8},{8,12},{12,16},{16,20},{20,24},{24,28},{28,32},{32,36}... | collective-permute-start | bytes 24584 | tf_op jit(solution)/shard_map/ppermute | solution.py:14
  205.7 2.6 convolution_bitcast_fusion
  210.3 9.2 %all_gather.7 = bf16[256,256]{1,0:T(8,128)(2,1)S(1)} all-gather(bf16[64,256]{1,0:T(8,128)(2,1)S(1)} %multiply_convert_fusion.2), channel_id=1, replica_groups=mesh['brick'=128,'ch'=4] {'ch'}, dimensions={0}, use_global_device_ids=true | all-gather | bytes 163840 | tf_op jit(solution)/shard_map/all_gather | solution.py:50
  222.8 2.5 copy.121
  225.2 39.1 %scatter_custom_fusion.4 = f32[64,320]{0,1:T(8,128)S(1)} fusion(s32[6912]{0:T(1024)} %copy-done.18, f32[6912,64]{1,0:T(8,128)} %bitcast.100, f32[]{:T(128)} %constant.44.clone.1), kind=kCustom, calls=%fused_computation.38 | custom fusion | flops 442368 | bytes 82432 | tf_op jit(solution)/shard_map/scatter-add | solution.py:56
  264.4 6.4 %collective-permute-start.6 = (f32[64,32]{0,1:T(8,128)S(1)}, f32[64,32]{0,1:T(8,128)S(1)}, u32[]{:S(2)}, u32[]{:S(2)}) collective-permute-start(f32[64,32]{0,1:T(8,128)S(1)} %get-tuple-element.43), channel_id=1, source_target_pairs={{0,4},{4,8},{8,12},{12,16},{16,20},{20,24},{24,28},{28,32},{32,36}... | collective-permute-start | bytes 24584 | tf_op jit(solution)/shard_map/ppermute | solution.py:14
  277.8 15.4 %all-to-all-start.2 = ((bf16[64,128,2]{0,2,1:T(2,128)(2,1)}), bf16[64,128,2]{0,2,1:T(2,128)(2,1)S(1)}, u32[]{:S(2)}, u32[]{:S(2)}) async-start(bf16[64,128,2]{0,2,1:T(2,128)(2,1)} %bitcast.36), calls=%async_computation.2 | async-start | bytes 131072 | tf_op jit(solution)/shard_map/all_to_all | solution.py:136
  293.3 11.4 %all-to-all-done.2 = bf16[64,128,2]{0,2,1:T(2,128)(2,1)S(1)} async-done(((bf16[64,128,2]{0,2,1:T(2,128)(2,1)}), bf16[64,128,2]{0,2,1:T(2,128)(2,1)S(1)}, u32[]{:S(2)}, u32[]{:S(2)}) %all-to-all-start.2) | async-done | bytes 32800 | tf_op jit(solution)/shard_map/all_to_all | solution.py:136
  306.2 122.7 %all-reduce.3.cloned.1.call-done = (f32[27,64,256]{2,1,0:T(8,128)}, f32[27,64,256]{2,1,0:T(8,128)}) async-done(((f32[27,64,256]{2,1,0:T(8,128)}, f32[27,64,256]{2,1,0:T(8,128)}), (f32[27,64,256]{2,1,0:T(8,128)}, f32[27,64,256]{2,1,0:T(8,128)})) %all-reduce.3.cloned.1.call-update) | async-done | bytes 3538960 | tf_op jit(solution)/shard_map/psum | solution.py:130
  428.9 3.7 multiply_convert_fusion
  (137 shorter events, 40.9 us)
Async XLA Ops:
  7.2 110.1 %copy-start = (bf16[27,64,256]{2,1,0:T(8,128)(2,1)S(1)}, bf16[27,64,256]{2,1,0:T(8,128)(2,1)}, u32[]{:S(2)}) copy-start(bf16[27,64,256]{2,1,0:T(8,128)(2,1)} %param.20) | copy-start | bytes 2654212
  13.1 29.9 %all-to-all-start = ((bf16[64,128,2]{0,2,1:T(2,128)(2,1)}), bf16[64,128,2]{0,2,1:T(2,128)(2,1)S(1)}, u32[]{:S(2)}, u32[]{:S(2)}) async-start(bf16[64,128,2]{0,2,1:T(2,128)(2,1)} %bitcast.4), calls=%async_computation | async-start | bytes 131072 | tf_op jit(solution)/shard_map/all_to_all | solution.py:95
  31.6 61.0 %reduce-scatter.7.cloned.1.call-start = ((), (), s32[]{:S(2)}) async-start(), calls=%async_computation.5 | async-start | bytes 327680 | tf_op jit(solution)/shard_map/reduce_scatter | solution.py:39
  34.0 31.3 %copy-start.19 = (s32[1024]{0:T(1024)}, s32[1024]{0:T(1024)S(1)}, u32[]{:S(2)}) copy-start(s32[1024]{0:T(1024)S(1)} %pad_clamp_fusion.2) | copy-start | bytes 12292
  43.7 5.5 %collective-permute-start = (bf16[64,32]{0,1:T(8,128)(2,1)S(1)}, bf16[64,32]{0,1:T(8,128)(2,1)S(1)}, u32[]{:S(2)}, u32[]{:S(2)}) collective-permute-start(bf16[64,32]{0,1:T(8,128)(2,1)S(1)} %select_bitcast_fusion.4), channel_id=1, source_target_pairs={{0,4},{4,8},{8,12},{12,16},{16,20},{20,24},{24,28},{28,32},{32,36}... | collective-permute-start | bytes 12296 | tf_op jit(solution)/shard_map/ppermute | solution.py:14
  47.3 5.0 %collective-permute-start.1 = (bf16[64,32]{0,1:T(8,128)(2,1)S(1)}, bf16[64,32]{0,1:T(8,128)(2,1)S(1)}, u32[]{:S(2)}, u32[]{:S(2)}) collective-permute-start(bf16[64,32]{0,1:T(8,128)(2,1)S(1)} %select_bitcast_fusion.3), channel_id=1, source_target_pairs={{4,0},{8,4},{12,8},{16,12},{20,16},{24,20},{28,24},{32,28},{36,32}... | collective-permute-start | bytes 12296 | tf_op jit(solution)/shard_map/ppermute | solution.py:17
  68.2 26.8 %copy-start.23 = (pred[32]{0:T(512)(128)(4,1)S(1)}, pred[32]{0:T(512)(128)(4,1)}, u32[]{:S(2)}) copy-start(pred[32]{0:T(512)(128)(4,1)} %copy-done.22) | copy-start | bytes 100
  68.3 29.8 %copy-start.21 = (pred[32]{0:T(512)(128)(4,1)S(1)}, pred[32]{0:T(512)(128)(4,1)}, u32[]{:S(2)}) copy-start(pred[32]{0:T(512)(128)(4,1)} %copy-done.20) | copy-start | bytes 100
  68.3 35.1 %copy-start.7 = (s32[7168]{0:T(1024)S(1)}, s32[7168]{0:T(1024)}, u32[]{:S(2)}) copy-start(s32[7168]{0:T(1024)} %copy-done.6) | copy-start | bytes 86020
  69.1 72.7 %reduce-scatter.9.cloned.1.call-start = ((), (), s32[]{:S(2)}) async-start(), calls=%async_computation.6 | async-start | bytes 327680 | tf_op jit(solution)/shard_map/reduce_scatter | solution.py:39
  95.0 5.0 %collective-permute-start.2 = (bf16[64,32]{1,0:T(8,128)(2,1)S(1)}, bf16[64,32]{1,0:T(8,128)(2,1)S(1)}, u32[]{:S(2)}, u32[]{:S(2)}) collective-permute-start(bf16[64,32]{1,0:T(8,128)(2,1)S(1)} %select_bitcast_fusion.2), channel_id=1, source_target_pairs={{0,4},{4,8},{8,12},{12,16},{16,20},{20,24},{24,28},{28,32},{32,36}... | collective-permute-start | bytes 12296 | tf_op jit(solution)/shard_map/ppermute | solution.py:14
  98.1 5.1 %collective-permute-start.3 = (bf16[64,32]{1,0:T(8,128)(2,1)S(1)}, bf16[64,32]{1,0:T(8,128)(2,1)S(1)}, u32[]{:S(2)}, u32[]{:S(2)}) collective-permute-start(bf16[64,32]{1,0:T(8,128)(2,1)S(1)} %select_bitcast_fusion.1), channel_id=1, source_target_pairs={{4,0},{8,4},{12,8},{16,12},{20,16},{24,20},{28,24},{32,28},{36,32}... | collective-permute-start | bytes 12296 | tf_op jit(solution)/shard_map/ppermute | solution.py:17
  118.7 310.2 %all-reduce.3.cloned.1.call-start = ((), (), s32[]{:S(2)}) async-start(), calls=%async_computation.7 | async-start | bytes 7077888 | tf_op jit(solution)/shard_map/psum | solution.py:130
  194.7 13.6 %collective-permute-start.4 = (f32[64,32]{0,1:T(8,128)S(1)}, f32[64,32]{0,1:T(8,128)S(1)}, u32[]{:S(2)}, u32[]{:S(2)}) collective-permute-start(f32[64,32]{0,1:T(8,128)S(1)} %get-tuple-element.45), channel_id=1, source_target_pairs={{0,4},{4,8},{8,12},{12,16},{16,20},{20,24},{24,28},{28,32},{32,36}... | collective-permute-start | bytes 24584 | tf_op jit(solution)/shard_map/ppermute | solution.py:14
  203.7 5.6 %collective-permute-start.5 = (f32[64,32]{0,1:T(8,128)S(1)}, f32[64,32]{0,1:T(8,128)S(1)}, u32[]{:S(2)}, u32[]{:S(2)}) collective-permute-start(f32[64,32]{0,1:T(8,128)S(1)} %get-tuple-element.44), channel_id=1, source_target_pairs={{4,0},{8,4},{12,8},{16,12},{20,16},{24,20},{28,24},{32,28},{36,32}... | collective-permute-start | bytes 24584 | tf_op jit(solution)/shard_map/ppermute | solution.py:17
  222.7 50.1 %copy-start.9 = (bf16[64,256]{1,0:T(8,128)(2,1)S(1)}, bf16[64,256]{1,0:T(8,128)(2,1)}, u32[]{:S(2)}) copy-start(bf16[64,256]{1,0:T(8,128)(2,1)} %copy-done.8) | copy-start | bytes 98308
  222.7 50.1 %copy-start.14 = (s32[64,256]{1,0:T(8,128)S(1)}, s32[64,256]{1,0:T(8,128)}, u32[]{:S(2)}) copy-start(s32[64,256]{1,0:T(8,128)} %param.18) | copy-start | bytes 196612
  222.8 50.1 %copy-start.15 = (f32[64,256]{1,0:T(8,128)S(1)}, f32[64,256]{1,0:T(8,128)}, u32[]{:S(2)}) copy-start(f32[64,256]{1,0:T(8,128)} %reduce-scatter.9.cloned.1.call-done) | copy-start | bytes 196612
  222.8 50.1 %copy-start.17 = (bf16[64,256]{1,0:T(8,128)(2,1)S(1)}, bf16[64,256]{1,0:T(8,128)(2,1)}, u32[]{:S(2)}) copy-start(bf16[64,256]{1,0:T(8,128)(2,1)} %param.21) | copy-start | bytes 98308
  225.2 68.0 %copy-start.27 = (s32[128,1]{0,1:T(1,128)S(1)}, s32[128,1]{0,1:T(1,128)}, u32[]{:S(2)}) copy-start(s32[128,1]{0,1:T(1,128)} %copy-done.26) | copy-start | bytes 1540
  225.2 80.2 %copy-start.25 = (pred[128]{0:T(512)(128)(4,1)S(1)}, pred[128]{0:T(512)(128)(4,1)}, u32[]{:S(2)}) copy-start(pred[128]{0:T(512)(128)(4,1)} %get-tuple-element.34) | copy-start | bytes 388
  264.4 9.2 %collective-permute-start.6 = (f32[64,32]{0,1:T(8,128)S(1)}, f32[64,32]{0,1:T(8,128)S(1)}, u32[]{:S(2)}, u32[]{:S(2)}) collective-permute-start(f32[64,32]{0,1:T(8,128)S(1)} %get-tuple-element.43), channel_id=1, source_target_pairs={{0,4},{4,8},{8,12},{12,16},{16,20},{20,24},{24,28},{28,32},{32,36}... | collective-permute-start | bytes 24584 | tf_op jit(solution)/shard_map/ppermute | solution.py:14
  270.9 5.5 %collective-permute-start.7 = (f32[64,32]{0,1:T(8,128)S(1)}, f32[64,32]{0,1:T(8,128)S(1)}, u32[]{:S(2)}, u32[]{:S(2)}) collective-permute-start(f32[64,32]{0,1:T(8,128)S(1)} %get-tuple-element.42), channel_id=1, source_target_pairs={{4,0},{8,4},{12,8},{16,12},{20,16},{24,20},{28,24},{32,28},{36,32}... | collective-permute-start | bytes 24584 | tf_op jit(solution)/shard_map/ppermute | solution.py:17
  277.8 26.9 %all-to-all-start.2 = ((bf16[64,128,2]{0,2,1:T(2,128)(2,1)}), bf16[64,128,2]{0,2,1:T(2,128)(2,1)S(1)}, u32[]{:S(2)}, u32[]{:S(2)}) async-start(bf16[64,128,2]{0,2,1:T(2,128)(2,1)} %bitcast.36), calls=%async_computation.2 | async-start | bytes 131072 | tf_op jit(solution)/shard_map/all_to_all | solution.py:136
  (18 other events, 219.4 us)
Sparse Core Ops, SparseCore 0:
  69.3 20.6 reduce-scatter.6
  118.8 23.0 reduce-scatter.8
  221.3 207.5 all-reduce.2
where the time goes:
time: 441 us; the launch traced here: 439 us
  waiting for transfers between devices  174 us (39%)
  other arithmetic  97.8 us (22%)
  starting transfers between devices  63 us (14%)
  local copies, waits for them, and re-layouts  42.5 us (10%)
  blocking collectives  39.1 us (9%)
  between operations  14.5 us (3%)
  matrix products  8.63 us (2%)
    psum x1, waiting for transfers between devices, local(): lax.psum((weight_grad_first, weight_grad_second), 'brick')  123 us
    scatter-add x2, other arithmetic, adjoint(): jnp.zeros((pushed.shape[0], extent), jnp.float32).at[:, kernel_map]  78.2 us
    gather x4, local copies, waits for them, and re-layouts, convolve(): gathered = jnp.take(extended, kernel_map, axis=1, mode='fill', fill_value=0)  27.8 us
    reduce_scatter x2, waiting for transfers between devices, convolve(): lax.psum_scatter(jnp.einsum('ckr,kco->or', gathered, weight, preferred_el...  22.5 us
    ppermute x4, starting transfers between devices, with_halo(): lax.ppermute(lax.slice_in_dim(block, block.shape[dim] - width, None, axis...  21.2 us
    all_to_all x1, blocking collectives, local(): lax.all_to_all(tallies, 'brick', split_axis=1, concat_axis=1, tiled=True)  20.6 us
    all_gather x2, blocking collectives, adjoint(): gathered_grad = lax.all_gather(grad_local, 'ch', axis=0, tiled=True)  18.5 us
    all_to_all x1, starting transfers between devices, local(): lax.all_to_all(outgoing.reshape(channels, bricks, capacity), 'brick', spl...  18.4 us
  transfers between devices with their start and end apart: 13, of which 7 were waited for; matrix products, arithmetic and copies ran while one was open for 13% of the time, Pallas kernels for 0%

commit v1 on v0

v1 whole, which is shorter than its diff:
```python
import functools

import jax
import jax.numpy as jnp
from jax import lax
from jax.experimental import pallas as pl
from jax.experimental.pallas import tpu as pltpu
from jax.sharding import PartitionSpec as P

KEEP_RATE = 0.9
MESH = pl.DeviceIdType.MESH
BF = jnp.bfloat16
F32 = jnp.float32
I32 = jnp.int32
CORES = 2
LANE = 128


def dot(a, b):
    return jnp.dot(a, b, preferred_element_type=F32)


def dot_nt(a, b):
    return lax.dot_general(a, b, (((1,), (1,)), ((), ())), preferred_element_type=F32)


def onehot(mask):
    return jnp.where(mask, 1.0, 0.0).astype(BF)


def iota(shape, dim):
    return lax.broadcasted_iota(I32, shape, dim)


def split(value):
    high = value.astype(BF)
    return high, (value - high.astype(F32)).astype(BF)


def slope_silu(value):
    sig = jax.nn.sigmoid(value)
    return sig * (1.0 + value * (1.0 - sig))


def loop(low, high, body):
    def step(index, carry):
        body(index)
        return carry

    lax.fori_loop(low, high, step, 0)


class Swap:
    def __init__(self, n, peer, src, dst, land, sems):
        self.n, self.peer, self.src, self.dst, self.land = n, peer, src, dst, land
        self.ss, self.rs = sems

    def _copy(self, d, src, dst):
        return pltpu.make_async_remote_copy(
            src_ref=src,
            dst_ref=dst,
            send_sem=self.ss.at[d - 1],
            recv_sem=self.rs.at[d - 1],
            device_id=self.peer(d),
            device_id_type=MESH,
        )

    def start(self):
        loop(1, self.n, lambda d: self._copy(d, self.src(d), self.dst(d)).start())

    def wait(self):
        loop(1, self.n, lambda d: self._copy(d, self.land(d), self.land(d)).wait_recv())

    def done(self):
        loop(1, self.n, lambda d: self._copy(d, self.src(d), self.dst(d)).wait_send())


def sizes(bricks, ys, koff, chans, outs):
    zs = bricks // CORES // ys
    rows = koff * chans
    unit = CORES * ys * 16
    padded = -(-rows // unit) * unit
    padded = -(-padded // LANE) * LANE
    half = padded // CORES
    first = half // ys
    second = -(-first // zs // 16) * 16 if first % zs == 0 else -(-first // (16 * zs)) * 16
    return zs, rows, padded, half, first, second


def kernel(
    dims,
    feat,
    owner,
    aux,
    kmap,
    drop1,
    drop2,
    w1,
    w2,
    cot,
    out_ref,
    gf_ref,
    wg1_ref,
    wg2_ref,
    oh,
    wt1,
    wt2,
    tab,
    gath1,
    gath2,
    pushed,
    ret,
    pm,
    em,
    perm,
    a_send,
    a_recv,
    b_send,
    b_recv,
    bb_send,
    bb_recv,
    ba_send,
    ba_recv,
    hs,
    hr,
    fs,
    fr,
    rs_send,
    rs_recv,
    full_g,
    wgf,
    wgb,
    c_recv,
    s1_src,
    s1_ra,
    s1_rb,
    s2_src,
    s2_ra,
    s2_rb,
    fin,
    chunk,
    halves,
    whole,
    *sems,
):
    bricks, ys, zs, chs, koff, chans, rows, padded, half, first, second, scale = dims
    qs = zs * CORES
    b, x = lax.axis_index("brick"), lax.axis_index("ch")
    y, q = b // qs, b % qs
    z, core = q // CORES, q % CORES
    slots = kmap.shape[1]
    sem_at = iter([(sems[i], sems[i + 1]) for i in range(0, len(sems), 2)])

    def ring(count, at, step):
        return lax.rem(at + step, count)

    to_y = lambda d: (ring(ys, y, d) * qs + q, x)
    to_q = lambda d: (y * qs + ring(qs, q, d), x)
    to_z = lambda d: (y * qs + ring(zs, z, d) * CORES + core, x)
    to_core = lambda d: (y * qs + z * CORES + (1 - core), x)
    to_ch = lambda d: (b, ring(chs, x, d))
    to_brick = lambda d: (lax.rem(b + 1 + (d - 1) * (bricks - 2), bricks), x)

    barrier = pltpu.get_barrier_semaphore()
    groups = ((to_y, ys), (to_q, qs), (to_ch, chs), (to_brick, 3))
    for peer, n in groups:
        loop(
            1,
            n,
            lambda d, peer=peer: pl.semaphore_signal(
                barrier, inc=1, device_id=peer(d), device_id_type=MESH
            ),
        )

    prows = 2 * bricks
    t_col, t_row = owner[...], aux[0:1, :]
    scan = t_row.shape[1]
    earlier = (t_col == t_row) & (iota((scan, scan), 0) < iota((scan, scan), 1))
    ordinal = jnp.sum(jnp.where(earlier, 1.0, 0.0), axis=0, keepdims=True)
    code = (t_row // qs) * (2 * qs) + ordinal.astype(I32) * qs + t_row % qs
    pm[...] = onehot(iota((prows, scan), 0) == code)
    carried = jnp.concatenate(
        [feat[...], jnp.where(iota((LANE - chans, scan), 0) == 0, 1.0, 0.0).astype(BF)], axis=0
    )
    a_send[...] = dot_nt(pm[...], carried).astype(BF)

    pl.semaphore_wait(barrier, sum(n - 1 for _, n in groups))

    def chunk_of(ref, index, size):
        return ref.at[pl.ds(pl.multiple_of(index * size, size), size)]

    ya, qa = 2 * qs, 2 * ys
    swap_a = Swap(
        ys,
        to_y,
        lambda d: chunk_of(a_send, ring(ys, y, d), ya),
        lambda d: chunk_of(a_recv, y, ya),
        lambda d: chunk_of(a_recv, ring(ys, y, ys - d), ya),
        next(sem_at),
    )
    swap_b = Swap(
        qs,
        to_q,
        lambda d: chunk_of(b_send, ring(qs, q, d), qa),
        lambda d: chunk_of(b_recv, q, qa),
        lambda d: chunk_of(b_recv, ring(qs, q, qs - d), qa),
        next(sem_at),
    )
    back_b = Swap(
        qs,
        to_q,
        lambda d: chunk_of(bb_send, ring(qs, q, d), qa),
        lambda d: chunk_of(bb_recv, q, qa),
        lambda d: chunk_of(bb_recv, ring(qs, q, qs - d), qa),
        next(sem_at),
    )
    back_a = Swap(
        ys,
        to_y,
        lambda d: chunk_of(ba_send, ring(ys, y, d), ya),
        lambda d: chunk_of(ba_recv, y, ya),
        lambda d: chunk_of(ba_recv, ring(ys, y, ys - d), ya),
        next(sem_at),
    )

    def neighbours(send, recv, at):
        return Swap(
            3,
            to_brick,
            lambda d: send.at[at, d - 1],
            lambda d: recv.at[at, d - 1],
            lambda d: recv.at[at, d - 1],
            next(sem_at),
        )

    halo1, halo2 = neighbours(hs, hr, 0), neighbours(hs, hr, 1)
    fold2, fold1 = neighbours(fs, fr, 0), neighbours(fs, fr, 1)

    def scatter_sum(at):
        return Swap(
            chs,
            to_ch,
            lambda d: chunk_of(rs_send.at[at], ring(chs, x, d), chans),
            lambda d: rs_recv.at[at, d - 1],
            lambda d: rs_recv.at[at, d - 1],
            next(sem_at),
        )

    sum1, sum2 = scatter_sum(0), scatter_sum(1)

    def share(at):
        return Swap(
            chs,
            to_ch,
            lambda d: chunk_of(full_g.at[at], x, chans),
            lambda d: chunk_of(full_g.at[at], x, chans),
            lambda d: chunk_of(full_g.at[at], ring(chs, x, chs - d), chans),
            next(sem_at),
        )

    share2, share1 = share(0), share(1)

    left, right = pl.ds(0, LANE), pl.ds(LANE, LANE)

    def rows_of(ref, start, size, lanes):
        return ref.at[pl.ds(pl.multiple_of(start, 16), size), lanes]

    def second_at(index):
        return jnp.minimum(index * second, first - second)

    class Total:
        def __init__(self, at):
            self.at = at
            other = (1 - core) * half
            self.cores = Swap(
                2,
                to_core,
                lambda d: wgb.at[at, pl.ds(pl.multiple_of(other, 16), half)],
                lambda d: c_recv.at[at],
                lambda d: c_recv.at[at],
                next(sem_at),
            )
            src = s1_src.at[at]
            self.first = (
                Swap(
                    ys,
                    to_y,
                    lambda d: rows_of(src, ring(ys, y, d) * first, first, left),
                    lambda d: s1_ra.at[at, d - 1],
                    lambda d: s1_ra.at[at, d - 1],
                    next(sem_at),
                ),
                Swap(
                    zs,
                    to_z,
                    lambda d: rows_of(src, ring(zs, z, d) * first, first, right),
                    lambda d: s1_rb.at[at, d - 1],
                    lambda d: s1_rb.at[at, d - 1],
                    next(sem_at),
                ),
            )
            self.second = (
                Swap(
                    zs,
                    to_z,
                    lambda d: s2_src.at[at, 0, pl.ds(pl.multiple_of(second_at(ring(zs, z, d)), 16), second)],
                    lambda d: s2_ra.at[at, d - 1],
                    lambda d: s2_ra.at[at, d - 1],
                    next(sem_at),
                ),
                Swap(
                    ys,
                    to_y,
                    lambda d: s2_src.at[at, 1, pl.ds(pl.multiple_of(second_at(ring(ys, y, d)), 16), second)],
                    lambda d: s2_rb.at[at, d - 1],
                    lambda d: s2_rb.at[at, d - 1],
                    next(sem_at),
                ),
            )
            self.third = (
                Swap(
                    zs,
                    to_z,
                    lambda d: fin.at[at, 0],
                    lambda d: chunk_of(chunk.at[at, 0], z, second),
                    lambda d: chunk_of(chunk.at[at, 0], ring(zs, z, zs - d), second),
                    next(sem_at),
                ),
                Swap(
                    ys,
                    to_y,
                    lambda d: fin.at[at, 1],
                    lambda d: chunk_of(chunk.at[at, 1], y, second),
                    lambda d: chunk_of(chunk.at[at, 1], ring(ys, y, ys - d), second),
                    next(sem_at),
                ),
            )
            dst = halves.at[at]
            self.fourth = (
                Swap(
                    ys,
                    to_y,
                    lambda d: chunk.at[at, 0, pl.ds(0, first)],
                    lambda d: rows_of(dst, y * first, first, left),
                    lambda d: rows_of(dst, ring(ys, y, ys - d) * first, first, left),
                    next(sem_at),
                ),
                Swap(
                    zs,
                    to_z,
                    lambda d: chunk.at[at, 1, pl.ds(0, first)],
                    lambda d: rows_of(dst, z * first, first, right),
                    lambda d: rows_of(dst, ring(zs, z, zs - d) * first, first, right),
                    next(sem_at),
                ),
            )
            self.last = Swap(
                2,
                to_core,
                lambda d: halves.at[at],
                lambda d: whole.at[at],
                lambda d: whole.at[at],
                next(sem_at),
            )
            self.all = (self.cores, *self.first, *self.second, *self.third, *self.fourth, self.last)

        def compute(self, gath, grads):
            at, block = self.at, half // 2
            g = grads[...]

            def step(i):
                span = pl.ds(pl.multiple_of(i * block, 16), block)
                part = dot_nt(gath[span, :], g)
                wgf[at, span, :] = part
                wgb[at, span, :] = part.astype(BF)

            loop(0, 2 * CORES, step)
            self.cores.start()

        def to_first(self):
            self.cores.wait()
            own = wgf[self.at, pl.ds(pl.multiple_of(core * half, 16), half), :]
            both = own + c_recv[self.at].astype(F32)
            s1_src[self.at] = both.astype(BF)
            for swap in self.first:
                swap.start()

        def to_second(self):
            for side, (swap, recv, pos, lanes, n) in enumerate(
                zip(self.first, (s1_ra, s1_rb), (y, z), (left, right), (ys, zs))
            ):
                swap.wait()
                span = pl.ds(pl.multiple_of(pos * first, 16), first)
                total = s1_src[self.at, span, lanes].astype(F32)
                for d in range(n - 1):
                    total = total + recv[self.at, d].astype(F32)
                s2_src[self.at, side] = total
                self.second[side].start()

        def to_third(self):
            for side, (swap, recv, pos, n) in enumerate(
                zip(self.second, (s2_ra, s2_rb), (z, y), (zs, ys))
            ):
                swap.wait()
                span = pl.ds(pl.multiple_of(second_at(pos), 16), second)
                total = s2_src[self.at, side, span, :]
                for d in range(n - 1):
                    total = total + recv[self.at, d]
                done = (total * scale).astype(BF)
                fin[self.at, side] = done
                chunk[self.at, side, pl.ds(pl.multiple_of(pos * second, 16), second), :] = done
                self.third[side].start()

        def to_fourth(self):
            for side, (swap, pos, lanes) in enumerate(zip(self.third, (y, z), (left, right))):
                swap.wait()
                self.fourth[side].start()
                span = pl.ds(pl.multiple_of(pos * first, 16), first)
                halves[self.at, span, lanes] = chunk[self.at, side, pl.ds(0, first), :]

        def to_last(self):
            for swap in self.fourth:
                swap.wait()
            self.last.start()

        def finish(self, ref):
            mine, theirs = halves[self.at], None
            self.last.wait()
            theirs = whole[self.at]
            upper = rows - half
            ref[0:half, :] = jnp.where(core == 0, mine, theirs)
            ref[half:rows, :] = jnp.where(core == 0, theirs, mine)[0:upper]

    total2, total1 = Total(0), Total(1)

    def own_rows(src, dst, index, size):
        span = pl.ds(pl.multiple_of(index * size, size), size)
        dst[span, :] = src[span, :]

    swap_a.start()
    own_rows(a_send, a_recv, y, ya)

    pr, pc = iota((prows, prows), 0), iota((prows, prows), 1)
    perm[...] = onehot(pc == (pr % ys) * ya + ((pr // ys) % 2) * qs + pr // qa)
    er, ec = iota((prows, slots), 0), iota((prows, slots), 1)
    em[...] = onehot(ec == 2 * ((er % ys) * qs + er // qa) + (er // ys) % 2)

    rim = 32

    def build(k):
        row = kmap[pl.ds(k, 1), :]
        inner = jnp.where(row < rim + slots, row - rim, row)
        column = jnp.where(row < rim, row + slots, jnp.where(row >= slots + 2 * rim, -1, inner))
        oh[k] = onehot(iota(oh.shape[1:], 0) == column)

    loop(0, koff // 3, build)

    swap_a.wait()
    b_send[...] = dot(perm[...], a_recv[...]).astype(BF)
    swap_b.start()
    own_rows(b_send, b_recv, q, qa)

    loop(koff // 3, koff, build)

    def turn(source, target):
        blocks = rows // LANE

        def step(j):
            at = pl.multiple_of(j * LANE, LANE)
            target[:, pl.ds(at, LANE)] = source[pl.ds(at, LANE), :].astype(F32).T.astype(BF)

        loop(0, blocks, step)
        if rows % LANE:
            tail = source[blocks * LANE : rows, :].astype(F32)
            tail = jnp.concatenate([tail, jnp.zeros((LANE - rows % LANE, tail.shape[1]), F32)], 0)
            target[:, blocks * LANE : (blocks + 1) * LANE] = tail.T.astype(BF)

    turn(w1, wt1)
    turn(w2, wt2)
    for gath in (gath1, gath2):
        gath[rows:padded, :] = jnp.zeros((padded - rows, slots), BF)

    lent = iota((slots, LANE), 0) == aux[1:2, :]
    side = iota((slots, LANE), 1) < rim
    lend_next, lend_prev = onehot(lent & side), onehot(lent & ~side)
    has_prev = (b > 0).astype(F32)
    has_next = (b < bricks - 1).astype(F32)

    swap_b.wait()
    arrived = dot(b_recv[...].astype(F32).T.astype(BF), em[...])
    occupied = arrived[chans : chans + 1, :]
    voxels = arrived[0:chans, :].astype(BF)
    keep1 = occupied * drop1[...].astype(F32) / KEEP_RATE
    keep2 = occupied * drop2[...].astype(F32) / KEEP_RATE

    def lend(field, halo, at):
        hs[at, 0] = dot(field, lend_next).astype(BF)
        hs[at, 1] = dot(field, lend_prev).astype(BF)
        halo.start()
        tab[:, 0:slots] = field

    def convolve(halo, at, gath, wt, summing):
        halo.wait()
        edge = hr[at, 0].astype(F32) * has_prev + hr[at, 1].astype(F32) * has_next
        tab[:, slots : slots + LANE] = edge.astype(BF)
        table = tab[...]

        def step(k):
            gath[pl.ds(pl.multiple_of(k * chans, 16), chans), :] = dot(table, oh[k]).astype(BF)

        loop(0, koff, step)
        rs_send[at] = dot(wt[...], gath[...])
        summing.start()
        own = rs_send[at, pl.ds(pl.multiple_of(x * chans, 16), chans), :]
        summing.wait()
        for d in range(chs - 1):
            own = own + rs_recv[at, d]
        return own

    lend(voxels, halo1, 0)
    conv1 = convolve(halo1, 0, gath1, wt1, sum1)
    hidden = (conv1 * jax.nn.sigmoid(conv1) * keep1).astype(BF)
    lend(hidden, halo2, 1)
    conv2 = convolve(halo2, 1, gath2, wt2, sum2)
    summed = voxels.astype(F32) + keep2 * conv2
    grad_pre = cot[...].astype(F32) * slope_silu(summed)
    mine = pl.ds(pl.multiple_of(x * chans, 16), chans)
    full_g[0, mine, :] = (grad_pre * keep2).astype(BF)
    share2.start()
    out_ref[...] = (summed * jax.nn.sigmoid(summed)).astype(BF)

    def push(weight, grads, fold, at):
        g = grads[...]

        def ahead(j):
            span = pl.ds(pl.multiple_of(j * 3 * chans, 16), 3 * chans)
            high, low = split(dot(weight[span, :], g))
            for i in range(3):
                part = slice(i * chans, (i + 1) * chans)
                pushed[3 * j + i, 0:chans, :] = high[part]
                pushed[3 * j + i, chans : 2 * chans, :] = low[part]

        loop(0, koff // 3, ahead)
        ret[...] = jnp.zeros_like(ret)

        def step(k):
            ret[...] += dot_nt(pushed[k], oh[k])

        loop(0, koff, step)
        border = ret[0:chans, slots : slots + LANE] + ret[chans : 2 * chans, slots : slots + LANE]
        fs[at, 0] = border
        fs[at, 1] = border
        fold.start()

    def folded(fold, at):
        own = ret[0:chans, 0:slots] + ret[chans : 2 * chans, 0:slots]
        fold.wait()
        for part in split(fr[at, 0] * has_prev):
            own = own + dot_nt(part, lend_prev)
        for part in split(fr[at, 1] * has_next):
            own = own + dot_nt(part, lend_next)
        return own

    share2.wait()
    push(w2, full_g.at[0], fold2, 0)
    total2.compute(gath2, full_g.at[0])
    grad_hidden = folded(fold2, 0)
    full_g[1, mine, :] = (grad_hidden * keep1 * slope_silu(conv1)).astype(BF)
    share1.start()
    total2.to_first()
    share1.wait()
    push(w1, full_g.at[1], fold1, 1)
    total1.compute(gath1, full_g.at[1])
    grad_voxels = (grad_pre + folded(fold1, 1)).astype(BF)
    wide = jnp.concatenate([grad_voxels, jnp.zeros((LANE - chans, slots), BF)], axis=0)
    bb_send[...] = dot_nt(em[...], wide).astype(BF)
    back_b.start()
    own_rows(bb_send, bb_recv, q, qa)
    total1.to_first()
    back_b.wait()
    perm_back = onehot(pc == (pr % qs) * qa + ((pr // qs) % 2) * ys + pr // ya)
    ba_send[...] = dot(perm_back, bb_recv[...]).astype(BF)
    back_a.start()
    own_rows(ba_send, ba_recv, y, ya)
    total2.to_second()
    back_a.wait()
    gf = dot(ba_recv[...].astype(F32).T.astype(BF), pm[...])
    gf_ref[...] = gf[0:chans, :].astype(BF)
    total1.to_second()
    total2.to_third()
    total1.to_third()
    total2.to_fourth()
    total1.to_fourth()
    total2.to_last()
    total1.to_last()
    total2.finish(wg2_ref)
    total1.finish(wg1_ref)

    for swap in (
        swap_a,
        swap_b,
        back_b,
        back_a,
        halo1,
        halo2,
        fold2,
        fold1,
        sum1,
        sum2,
        share2,
        share1,
        *total2.all,
        *total1.all,
    ):
        swap.done()


def local(ys, features, owner_map, kernel_map, send_lists, drop1, drop2, w1, w2, cotangent):
    bricks, chs = lax.axis_size("brick"), lax.axis_size("ch")
    chans, scan = features.shape
    koff, slots = kernel_map.shape
    outs = w1.shape[2]
    zs, rows, padded, half, first, second = sizes(bricks, ys, koff, chans, outs)
    qs = zs * CORES
    rim = send_lists.shape[1]
    dims = (
        bricks, ys, zs, chs, koff, chans, rows, padded, half, first, second,
        float(bricks * slots) ** -0.5,
    )
    lists = jnp.concatenate(
        [send_lists[1:2], send_lists[0:1], jnp.full((1, LANE - 2 * rim), -1, I32)], axis=1
    )
    aux = jnp.concatenate([owner_map.reshape(1, scan), lists], axis=0)
    prows = 2 * bricks
    vm = pltpu.VMEM
    table = slots + LANE
    scratch = [
        vm((koff, table, slots), BF),
        vm((outs, padded), BF),
        vm((outs, padded), BF),
        vm((chans, table), BF),
        vm((padded, slots), BF),
        vm((padded, slots), BF),
        vm((koff, 2 * chans, slots), BF),
        vm((2 * chans, table), F32),
        vm((prows, scan), BF),
        vm((prows, slots), BF),
        vm((prows, prows), BF),
        *[vm((prows, LANE), BF)] * 8,
        vm((2, 2, chans, LANE), BF),
        vm((2, 2, chans, LANE), BF),
        vm((2, 2, chans, LANE), F32),
        vm((2, 2, chans, LANE), F32),
        vm((2, outs, slots), F32),
        vm((2, chs - 1, chans, slots), F32),
        vm((2, outs, slots), BF),
        vm((2, padded, outs), F32),
        vm((2, padded, outs), BF),
        vm((2, half, outs), BF),
        vm((2, half, outs), BF),
        vm((2, ys - 1, first, LANE), BF),
        vm((2, zs - 1, first, LANE), BF),
        vm((2, 2, first, LANE), F32),
        vm((2, zs - 1, second, LANE), F32),
        vm((2, ys - 1, second, LANE), F32),
        vm((2, 2, second, LANE), BF),
        vm((2, 2, max(ys, zs) * second, LANE), BF),
        vm((2, half, outs), BF),
        vm((2, half, outs), BF),
    ]
    weight_sums = [1, ys - 1, zs - 1, zs - 1, ys - 1, zs - 1, ys - 1, ys - 1, zs - 1, 1]
    copies = [ys - 1, qs - 1, qs - 1, ys - 1, 2, 2, 2, 2] + [chs - 1] * 4 + weight_sums * 2
    for n in copies:
        scratch += [pltpu.SemaphoreType.DMA((n,))] * 2
    shape = jax.ShapeDtypeStruct
    spec = pl.BlockSpec(memory_space=pltpu.VMEM)
    block_out, grad_features, wg1, wg2 = pl.pallas_call(
        functools.partial(kernel, dims),
        out_shape=(
            shape((chans, slots), BF),
            shape((chans, scan), BF),
            shape((rows, outs), BF),
            shape((rows, outs), BF),
        ),
        in_specs=[spec] * 9,
        out_specs=(spec,) * 4,
        scratch_shapes=scratch,
        compiler_params=pltpu.CompilerParams(
            collective_id=0, has_side_effects=True, vmem_limit_bytes=56 * 2**20
        ),
        name="block",
    )(
        features, owner_map, aux, kernel_map, drop1, drop2,
        w1.reshape(rows, outs), w2.reshape(rows, outs), cotangent,
    )
    return block_out, grad_features, wg1.reshape(w1.shape), wg2.reshape(w2.shape)


def rows_of_chips(bricks):
    ys = 1
    while ys * ys * CORES < bricks:
        ys *= 2
    return ys


def solution(mesh):
    return jax.shard_map(
        functools.partial(local, rows_of_chips(mesh.shape["brick"])),
        mesh=mesh,
        in_specs=(
            P("ch", "brick"),
            P("brick", None),
            P(None, "brick"),
            P(None, "brick"),
            P("ch", "brick"),
            P("ch", "brick"),
            P(None, "ch", None),
            P(None, "ch", None),
            P("ch", "brick"),
        ),
        out_specs=(P("ch", "brick"), P("ch", "brick"), P(None, "ch", None), P(None, "ch", None)),
        check_vma=False,
    )
```

time: 441 us -> 131 us (0.30)
  waiting for transfers between devices: 174 us -> 0 us
  Pallas kernels: 0 us -> 122 us
  other arithmetic: 97.8 us -> 0.64 us
  starting transfers between devices: 63 us -> 0 us
  blocking collectives: 39.1 us -> 0 us
  local copies, waits for them, and re-layouts: 42.5 us -> 7.23 us
  between operations: 14.5 us -> 0.66 us
  matrix products: 8.63 us -> 0 us
    psum x1 -> x0, waiting for transfers between devices: 123 us -> none  [local(): lax.psum((weight_grad_first, weight_grad_second), 'brick')]
    pallas_call x0 -> x1, Pallas kernels: none -> 122 us  [local(): pl.pallas_call(functools.partial(kernel, dims), out_shape=(shape((chans,...]
    scatter-add x6 -> x0, other arithmetic: 81.6 us -> none  [the longest x2 78.2 us: adjoint(): jnp.zeros((pushed.shape[0], extent), jnp.float32).at[:, kernel_map]]
    all_to_all x2 -> x0, starting transfers between devices: 33.9 us -> none  [the longest x1 18.4 us: local(): lax.all_to_all(outgoing.reshape(channels, bricks, capacity), 'brick', spl...]
    gather x11 -> x0, local copies, waits for them, and re-layouts: 31.2 us -> none  [the longest x4 27.8 us: convolve(): gathered = jnp.take(extended, kernel_map, axis=1, mode='fill', fill_value=0)]
    ppermute x8 -> x0, starting transfers between devices: 29 us -> none  [the longest x4 21.2 us: with_halo(): lax.ppermute(lax.slice_in_dim(block, block.shape[dim] - width, None, axis...]
    reduce_scatter x2 -> x0, waiting for transfers between devices: 22.5 us -> none  [convolve(): lax.psum_scatter(jnp.einsum('ckr,kco->or', gathered, weight, preferred_el...]
    all_to_all x1 -> x0, blocking collectives: 20.6 us -> none  [local(): lax.all_to_all(tallies, 'brick', split_axis=1, concat_axis=1, tiled=True)]
  transfers between devices with their start and end apart: 13 -> 0, of which waited for: 7 -> 0; matrix products, arithmetic and copies ran while one was open for 13% -> 0% of each run, Pallas kernels for 0% -> 0%
where the time goes in v1:
time: 131 us
  Pallas kernels  122 us (93%)
  local copies, waits for them, and re-layouts  7.23 us (6%)
    pallas_call x1, Pallas kernels, local(): pl.pallas_call(functools.partial(kernel, dims), out_shape=(shape((chans,...  122 us
    unnamed x13, local copies, waits for them, and re-layouts  7.22 us

profile of v1, /device:TPU:1, one launch (start us, length us, event | category | flops | bytes accessed | tf_op | source)
XLA Modules:
  0.0 130.9 jit_solution(13414381002221719636)
XLA Ops:
  0.6 0.0 copy-start.3
  0.6 0.7 copy-done.3
  1.3 0.0 copy-start.2
  1.3 0.7 copy-done.2
  2.0 0.6 add_add_fusion.aux
  2.6 0.7 copy.13.owner
  3.4 122.3 %block.1 = (bf16[64,256]{1,0:T(8,128)(2,1)}, bf16[64,128]{1,0:T(8,128)(2,1)}, bf16[1728,256]{1,0:T(8,128)(2,1)}, bf16[1728,256]{1,0:T(8,128)(2,1)}) custom-call(bf16[64,128]{1,0:T(8,128)(2,1)} %feat.1, s32[128,1]{1,0:T(8,128)} %copy.13.owner, s32[2,128]{1,0:T(2,128)} %add_add_fusion.aux, s32[27,256]{1,0:T(8,128)} %kmap.1, s32[64,256]{1,0:T(8,128)} %drop1.1, ...), custom_call_target="tpu_custom_call" | custom-call | tf_op jit(solution)/shard_map/block/pallas_call | solution.py:677
  125.7 0.0 copy-start.1
  125.7 1.4 %copy.18 = bf16[64,256]{1,0:T(8,128)(2,1)} copy(bf16[64,256]{1,0:T(8,128)(2,1)} %get-tuple-element.18) | data formatting | bytes 65536
  127.1 0.0 copy-done.1
  127.1 0.6 copy.19
  127.7 0.0 copy-start
  127.7 2.3 %copy.20 = bf16[27,64,256]{2,1,0:T(8,128)(2,1)} copy(bf16[27,64,256]{2,1,0:T(8,128)(2,1)} %bitcast.8) | data formatting | bytes 1769472
  130.0 0.0 copy-done
  130.0 0.9 copy.21
  (2 shorter events, 0.0 us)
Async XLA Ops:
  0.6 0.7 copy-start.3
  1.3 0.7 copy-start.2
  125.7 1.4 %copy-start.1 = (bf16[64,128]{1,0:T(8,128)(2,1)S(1)}, bf16[64,128]{1,0:T(8,128)(2,1)}, u32[]{:S(2)}) copy-start(bf16[64,128]{1,0:T(8,128)(2,1)} %get-tuple-element.19) | copy-start | bytes 49156
  127.7 2.3 %copy-start = (bf16[1728,256]{1,0:T(8,128)(2,1)S(1)}, bf16[1728,256]{1,0:T(8,128)(2,1)}, u32[]{:S(2)}) copy-start(bf16[1728,256]{1,0:T(8,128)(2,1)} %get-tuple-element.11) | copy-start | bytes 2654212

commit v2 on v1

--- a/solution.py
+++ b/solution.py
@@ -48,6 +48,11 @@
         return carry
 
     lax.fori_loop(low, high, step, 0)
+
+
+def unrolled(low, high, body):
+    for index in range(low, high):
+        body(index)
 
 
 class Swap:
@@ -65,11 +70,17 @@
             device_id_type=MESH,
         )
 
+    def start_one(self, d):
+        self._copy(d, self.src(d), self.dst(d)).start()
+
+    def wait_one(self, d):
+        self._copy(d, self.land(d), self.land(d)).wait_recv()
+
     def start(self):
-        loop(1, self.n, lambda d: self._copy(d, self.src(d), self.dst(d)).start())
+        loop(1, self.n, self.start_one)
 
     def wait(self):
-        loop(1, self.n, lambda d: self._copy(d, self.land(d), self.land(d)).wait_recv())
+        loop(1, self.n, self.wait_one)
 
     def done(self):
         loop(1, self.n, lambda d: self._copy(d, self.src(d), self.dst(d)).wait_send())
@@ -91,7 +102,7 @@
     dims,
     feat,
     owner,
-    aux,
+    lists,
     kmap,
     drop1,
     drop2,
@@ -139,8 +150,6 @@
     s2_rb,
     fin,
     chunk,
-    halves,
-    whole,
     *sems,
 ):
     bricks, ys, zs, chs, koff, chans, rows, padded, half, first, second, scale = dims
@@ -173,8 +182,9 @@
         )
 
     prows = 2 * bricks
-    t_col, t_row = owner[...], aux[0:1, :]
+    t_row = owner[...]
     scan = t_row.shape[1]
+    t_col = jnp.broadcast_to(t_row.astype(F32), (scan, scan)).T.astype(I32)
     earlier = (t_col == t_row) & (iota((scan, scan), 0) < iota((scan, scan), 1))
     ordinal = jnp.sum(jnp.where(earlier, 1.0, 0.0), axis=0, keepdims=True)
     code = (t_row // qs) * (2 * qs) + ordinal.astype(I32) * qs + t_row % qs
@@ -269,13 +279,12 @@
         return jnp.minimum(index * second, first - second)
 
     class Total:
-        def __init__(self, at):
-            self.at = at
-            other = (1 - core) * half
+        def __init__(self, at, ref):
+            self.at, self.ref = at, ref
             self.cores = Swap(
                 2,
                 to_core,
-                lambda d: wgb.at[at, pl.ds(pl.multiple_of(other, 16), half)],
+                lambda d: wgb.at[at],
                 lambda d: c_recv.at[at],
                 lambda d: c_recv.at[at],
                 next(sem_at),
@@ -335,52 +344,66 @@
                     next(sem_at),
                 ),
             )
-            dst = halves.at[at]
             self.fourth = (
                 Swap(
                     ys,
                     to_y,
                     lambda d: chunk.at[at, 0, pl.ds(0, first)],
-                    lambda d: rows_of(dst, y * first, first, left),
-                    lambda d: rows_of(dst, ring(ys, y, ys - d) * first, first, left),
+                    lambda d: rows_of(ref, core * half + y * first, first, left),
+                    lambda d: rows_of(ref, core * half + ring(ys, y, ys - d) * first, first, left),
                     next(sem_at),
                 ),
                 Swap(
                     zs,
                     to_z,
                     lambda d: chunk.at[at, 1, pl.ds(0, first)],
-                    lambda d: rows_of(dst, z * first, first, right),
-                    lambda d: rows_of(dst, ring(zs, z, zs - d) * first, first, right),
+                    lambda d: rows_of(ref, core * half + z * first, first, right),
+                    lambda d: rows_of(ref, core * half + ring(zs, z, zs - d) * first, first, right),
                     next(sem_at),
                 ),
             )
-            self.last = Swap(
-                2,
-                to_core,
-                lambda d: halves.at[at],
-                lambda d: whole.at[at],
-                lambda d: whole.at[at],
-                next(sem_at),
+            self.last = tuple(
+                Swap(
+                    n + 1,
+                    lambda d: to_core(1),
+                    lambda d, n=n, pos=pos, lanes=lanes: rows_of(
+                        ref, core * half + ring(n, pos, n + 1 - d) * first, first, lanes
+                    ),
+                    lambda d, n=n, pos=pos, lanes=lanes: rows_of(
+                        ref, core * half + ring(n, pos, n + 1 - d) * first, first, lanes
+                    ),
+                    lambda d, n=n, pos=pos, lanes=lanes: rows_of(
+                        ref, (1 - core) * half + ring(n, pos, n + 1 - d) * first, first, lanes
+                    ),
+                    next(sem_at),
+                )
+                for n, pos, lanes in ((ys, y, left), (zs, z, right))
             )
-            self.all = (self.cores, *self.first, *self.second, *self.third, *self.fourth, self.last)
+            self.all = (
+                self.cores, *self.first, *self.second, *self.third, *self.fourth, *self.last
+            )
 
         def compute(self, gath, grads):
-            at, block = self.at, half // 2
-            g = grads[...]
-
-            def step(i):
-                span = pl.ds(pl.multiple_of(i * block, 16), block)
+            at, g, block = self.at, grads[...], half // 2
+
+            def step(start, keep):
+                span = pl.ds(pl.multiple_of(start, 16), block)
                 part = dot_nt(gath[span, :], g)
-                wgf[at, span, :] = part
-                wgb[at, span, :] = part.astype(BF)
-
-            loop(0, 2 * CORES, step)
+                if keep:
+                    wgf[at, pl.ds(pl.multiple_of(start - core * half, 16), block), :] = part
+                else:
+                    at_b = pl.ds(pl.multiple_of(start - (1 - core) * half, 16), block)
+                    wgb[at, at_b, :] = part.astype(BF)
+
+            for i in range(2):
+                step((1 - core) * half + i * block, False)
             self.cores.start()
+            for i in range(2):
+                step(core * half + i * block, True)
 
         def to_first(self):
             self.cores.wait()
-            own = wgf[self.at, pl.ds(pl.multiple_of(core * half, 16), half), :]
-            both = own + c_recv[self.at].astype(F32)
+            both = wgf[self.at] + c_recv[self.at].astype(F32)
             s1_src[self.at] = both.astype(BF)
             for swap in self.first:
                 swap.start()
@@ -415,23 +438,24 @@
             for side, (swap, pos, lanes) in enumerate(zip(self.third, (y, z), (left, right))):
                 swap.wait()
                 self.fourth[side].start()
-                span = pl.ds(pl.multiple_of(pos * first, 16), first)
-                halves[self.at, span, lanes] = chunk[self.at, side, pl.ds(0, first), :]
+                span = pl.ds(pl.multiple_of(core * half + pos * first, 16), first)
+                self.ref[span, lanes] = chunk[self.at, side, pl.ds(0, first), :]
+                self.last[side].start_one(1)
 
         def to_last(self):
-            for swap in self.fourth:
+            for side, swap in enumerate(self.fourth):
+
+                def forward(d, swap=swap, side=side):
+                    swap.wait_one(d)
+                    self.last[side].start_one(d + 1)
+
+                loop(1, swap.n, forward)
+
+        def finish(self):
+            for swap in self.last:
                 swap.wait()
-            self.last.start()
-
-        def finish(self, ref):
-            mine, theirs = halves[self.at], None
-            self.last.wait()
-            theirs = whole[self.at]
-            upper = rows - half
-            ref[0:half, :] = jnp.where(core == 0, mine, theirs)
-            ref[half:rows, :] = jnp.where(core == 0, theirs, mine)[0:upper]
-
-    total2, total1 = Total(0), Total(1)
+
+    total2, total1 = Total(0, wg2_ref), Total(1, wg1_ref)
 
     def own_rows(src, dst, index, size):
         span = pl.ds(pl.multiple_of(index * size, size), size)
@@ -453,14 +477,14 @@
         column = jnp.where(row < rim, row + slots, jnp.where(row >= slots + 2 * rim, -1, inner))
         oh[k] = onehot(iota(oh.shape[1:], 0) == column)
 
-    loop(0, koff // 3, build)
+    unrolled(0, koff // 3, build)
 
     swap_a.wait()
     b_send[...] = dot(perm[...], a_recv[...]).astype(BF)
     swap_b.start()
     own_rows(b_send, b_recv, q, qa)
 
-    loop(koff // 3, koff, build)
+    unrolled(koff // 3, koff, build)
 
     def turn(source, target):
         blocks = rows // LANE
@@ -469,7 +493,7 @@
             at = pl.multiple_of(j * LANE, LANE)
             target[:, pl.ds(at, LANE)] = source[pl.ds(at, LANE), :].astype(F32).T.astype(BF)
 
-        loop(0, blocks, step)
+        unrolled(0, blocks, step)
         if rows % LANE:
             tail = source[blocks * LANE : rows, :].astype(F32)
             tail = jnp.concatenate([tail, jnp.zeros((LANE - rows % LANE, tail.shape[1]), F32)], 0)
@@ -480,7 +504,10 @@
     for gath in (gath1, gath2):
         gath[rows:padded, :] = jnp.zeros((padded - rows, slots), BF)
 
-    lent = iota((slots, LANE), 0) == aux[1:2, :]
+    both = jnp.concatenate(
+        [lists[1:2, :], lists[0:1, :], jnp.full((1, LANE - 2 * rim), -1, I32)], axis=1
+    )
+    lent = iota((slots, LANE), 0) == both
     side = iota((slots, LANE), 1) < rim
     lend_next, lend_prev = onehot(lent & side), onehot(lent & ~side)
     has_prev = (b > 0).astype(F32)
@@ -508,7 +535,7 @@
         def step(k):
             gath[pl.ds(pl.multiple_of(k * chans, 16), chans), :] = dot(table, oh[k]).astype(BF)
 
-        loop(0, koff, step)
+        unrolled(0, koff, step)
         rs_send[at] = dot(wt[...], gath[...])
         summing.start()
         own = rs_send[at, pl.ds(pl.multiple_of(x * chans, 16), chans), :]
@@ -540,13 +567,16 @@
                 pushed[3 * j + i, 0:chans, :] = high[part]
                 pushed[3 * j + i, chans : 2 * chans, :] = low[part]
 
-        loop(0, koff // 3, ahead)
+        unrolled(0, koff // 3, ahead)
         ret[...] = jnp.zeros_like(ret)
 
         def step(k):
-            ret[...] += dot_nt(pushed[k], oh[k])
-
-        loop(0, koff, step)
+            part = dot_nt(pushed[9 * k], oh[9 * k])
+            for i in range(9 * k + 1, 9 * k + 9):
+                part = part + dot_nt(pushed[i], oh[i])
+            ret[...] += part
+
+        unrolled(0, koff // 9, step)
         border = ret[0:chans, slots : slots + LANE] + ret[chans : 2 * chans, slots : slots + LANE]
         fs[at, 0] = border
         fs[at, 1] = border
@@ -569,8 +599,8 @@
     share1.start()
     total2.to_first()
     share1.wait()
+    total1.compute(gath1, full_g.at[1])
     push(w1, full_g.at[1], fold1, 1)
-    total1.compute(gath1, full_g.at[1])
     grad_voxels = (grad_pre + folded(fold1, 1)).astype(BF)
     wide = jnp.concatenate([grad_voxels, jnp.zeros((LANE - chans, slots), BF)], axis=0)
     bb_send[...] = dot_nt(em[...], wide).astype(BF)
@@ -593,8 +623,8 @@
     total1.to_fourth()
     total2.to_last()
     total1.to_last()
-    total2.finish(wg2_ref)
-    total1.finish(wg1_ref)
+    total2.finish()
+    total1.finish()
 
     for swap in (
         swap_a,
@@ -615,6 +645,18 @@
         swap.done()
 
 
+def store(*refs):
+    sources, targets, sem = refs[0:4], refs[4:8], refs[8]
+    copies = [
+        pltpu.make_async_copy(source.at[pl.ds(0, target.shape[0])], target, sem.at[i])
+        for i, (source, target) in enumerate(zip(sources, targets))
+    ]
+    for copy in copies:
+        copy.start()
+    for copy in copies:
+        copy.wait()
+
+
 def local(ys, features, owner_map, kernel_map, send_lists, drop1, drop2, w1, w2, cotangent):
     bricks, chs = lax.axis_size("brick"), lax.axis_size("ch")
     chans, scan = features.shape
@@ -627,10 +669,6 @@
         bricks, ys, zs, chs, koff, chans, rows, padded, half, first, second,
         float(bricks * slots) ** -0.5,
     )
-    lists = jnp.concatenate(
-        [send_lists[1:2], send_lists[0:1], jnp.full((1, LANE - 2 * rim), -1, I32)], axis=1
-    )
-    aux = jnp.concatenate([owner_map.reshape(1, scan), lists], axis=0)
     prows = 2 * bricks
     vm = pltpu.VMEM
     table = slots + LANE
@@ -654,8 +692,8 @@
         vm((2, outs, slots), F32),
         vm((2, chs - 1, chans, slots), F32),
         vm((2, outs, slots), BF),
-        vm((2, padded, outs), F32),
-        vm((2, padded, outs), BF),
+        vm((2, half, outs), F32),
+        vm((2, half, outs), BF),
         vm((2, half, outs), BF),
         vm((2, half, outs), BF),
         vm((2, ys - 1, first, LANE), BF),
@@ -665,22 +703,20 @@
         vm((2, ys - 1, second, LANE), F32),
         vm((2, 2, second, LANE), BF),
         vm((2, 2, max(ys, zs) * second, LANE), BF),
-        vm((2, half, outs), BF),
-        vm((2, half, outs), BF),
     ]
-    weight_sums = [1, ys - 1, zs - 1, zs - 1, ys - 1, zs - 1, ys - 1, ys - 1, zs - 1, 1]
+    weight_sums = [1, ys - 1, zs - 1, zs - 1, ys - 1, zs - 1, ys - 1, ys - 1, zs - 1, ys, zs]
     copies = [ys - 1, qs - 1, qs - 1, ys - 1, 2, 2, 2, 2] + [chs - 1] * 4 + weight_sums * 2
     for n in copies:
         scratch += [pltpu.SemaphoreType.DMA((n,))] * 2
     shape = jax.ShapeDtypeStruct
     spec = pl.BlockSpec(memory_space=pltpu.VMEM)
-    block_out, grad_features, wg1, wg2 = pl.pallas_call(
+    results = pl.pallas_call(
         functools.partial(kernel, dims),
         out_shape=(
             shape((chans, slots), BF),
             shape((chans, scan), BF),
-            shape((rows, outs), BF),
-            shape((rows, outs), BF),
+            shape((padded, outs), BF),
+            shape((padded, outs), BF),
         ),
         in_specs=[spec] * 9,
         out_specs=(spec,) * 4,
@@ -690,9 +726,23 @@
         ),
         name="block",
     )(
-        features, owner_map, aux, kernel_map, drop1, drop2,
+        features, owner_map.reshape(1, scan), send_lists, kernel_map, drop1, drop2,
         w1.reshape(rows, outs), w2.reshape(rows, outs), cotangent,
     )
+    anywhere = pl.BlockSpec(memory_space=pl.ANY)
+    block_out, grad_features, wg1, wg2 = pl.pallas_call(
+        store,
+        out_shape=(
+            shape((chans, slots), BF),
+            shape((chans, scan), BF),
+            shape((rows, outs), BF),
+            shape((rows, outs), BF),
+        ),
+        in_specs=[spec] * 4,
+        out_specs=(anywhere,) * 4,
+        scratch_shapes=[pltpu.SemaphoreType.DMA((4,))],
+        name="store",
+    )(*results)
     return block_out, grad_features, wg1.reshape(w1.shape), wg2.reshape(w2.shape)
 
 

time: 131 us -> 109 us (0.83)
  Pallas kernels: 122 us -> 108 us
  local copies, waits for them, and re-layouts: 7.23 us -> 0 us
    pallas_call x1, Pallas kernels: 122 us -> 105 us  [local(): pl.pallas_call(functools.partial(kernel, dims), out_shape=(shape((chans,...]
    unnamed x13 -> x0, local copies, waits for them, and re-layouts: 7.22 us -> none
    pallas_call x0 -> x1, Pallas kernels: none -> 2.75 us  [local(): pl.pallas_call(store, out_shape=(shape((chans, slots), BF), shape((chans,...]
where the time goes in v2:
time: 109 us; the launch traced here: 108 us
  Pallas kernels  108 us (99%)
    pallas_call x1, Pallas kernels, local(): pl.pallas_call(functools.partial(kernel, dims), out_shape=(shape((chans,...  105 us
    pallas_call x1, Pallas kernels, local(): pl.pallas_call(store, out_shape=(shape((chans, slots), BF), shape((chans,...  2.75 us

profile of v2, /device:TPU:1, one launch (start us, length us, event | category | flops | bytes accessed | tf_op | source)
XLA Modules:
  0.0 108.5 jit_solution(4441005191924749794)
XLA Ops:
  0.6 105.1 %block.1 = (bf16[64,256]{1,0:T(8,128)(2,1)}, bf16[64,128]{1,0:T(8,128)(2,1)}, bf16[1792,256]{1,0:T(8,128)(2,1)}, bf16[1792,256]{1,0:T(8,128)(2,1)}) custom-call(bf16[64,128]{1,0:T(8,128)(2,1)} %feat.1, s32[1,128]{1,0:T(1,128)} %bitcast.7, s32[2,32]{1,0:T(2,128)} %lists.1, s32[27,256]{1,0:T(8,128)} %kmap.1, s32[64,256]{1,0:T(8,128)} %drop1.1, ...), custom_call_target="tpu_custom_call" | custom-call | tf_op jit(solution)/shard_map/block/pallas_call | solution.py:713
  105.7 2.7 %store.1 = (bf16[64,256]{1,0:T(8,128)(2,1)}, bf16[64,128]{1,0:T(8,128)(2,1)}, bf16[1728,256]{1,0:T(8,128)(2,1)}, bf16[1728,256]{1,0:T(8,128)(2,1)}) custom-call(bf16[64,256]{1,0:T(8,128)(2,1)} %get-tuple-element.12.refs_0_, bf16[64,128]{1,0:T(8,128)(2,1)} %get-tuple-element.13.refs_1_, bf16[1792,256]{1,0:T(8,128)(2,1)} %get-tuple-element.14.refs_2_, ...), custom_call_target="tpu_custom_call" | custom-call | tf_op jit(solution)/shard_map/store/pallas_call | solution.py:733

commit v3 on v2

--- a/solution.py
+++ b/solution.py
@@ -77,10 +77,10 @@
         self._copy(d, self.land(d), self.land(d)).wait_recv()
 
     def start(self):
-        loop(1, self.n, self.start_one)
+        unrolled(1, self.n, self.start_one)
 
     def wait(self):
-        loop(1, self.n, self.wait_one)
+        unrolled(1, self.n, self.wait_one)
 
     def done(self):
         loop(1, self.n, lambda d: self._copy(d, self.src(d), self.dst(d)).wait_send())
@@ -116,7 +116,6 @@
     oh,
     wt1,
     wt2,
-    tab,
     gath1,
     gath2,
     pushed,
@@ -383,23 +382,22 @@
                 self.cores, *self.first, *self.second, *self.third, *self.fourth, *self.last
             )
 
-        def compute(self, gath, grads):
-            at, g, block = self.at, grads[...], half // 2
-
-            def step(start, keep):
-                span = pl.ds(pl.multiple_of(start, 16), block)
-                part = dot_nt(gath[span, :], g)
-                if keep:
-                    wgf[at, pl.ds(pl.multiple_of(start - core * half, 16), block), :] = part
-                else:
-                    at_b = pl.ds(pl.multiple_of(start - (1 - core) * half, 16), block)
-                    wgb[at, at_b, :] = part.astype(BF)
-
+        def compute(self, gath, grads, which):
+            g, block = grads[...], half // 2
             for i in range(2):
-                step((1 - core) * half + i * block, False)
+                start = which * half + i * block
+                yield pl.ds(i * block, block), dot_nt(
+                    gath[pl.ds(pl.multiple_of(start, 16), block), :], g
+                )
+
+        def give(self, gath, grads):
+            for span, part in self.compute(gath, grads, 1 - core):
+                wgb[self.at, span, :] = part.astype(BF)
             self.cores.start()
-            for i in range(2):
-                step(core * half + i * block, True)
+
+        def keep(self, gath, grads):
+            for span, part in self.compute(gath, grads, core):
+                wgf[self.at, span, :] = part
 
         def to_first(self):
             self.cores.wait()
@@ -524,18 +522,21 @@
         hs[at, 0] = dot(field, lend_next).astype(BF)
         hs[at, 1] = dot(field, lend_prev).astype(BF)
         halo.start()
-        tab[:, 0:slots] = field
-
-    def convolve(halo, at, gath, wt, summing):
+
+    def convolve(field, halo, at, gath, wt, summing):
+        def inner(k):
+            gath[k * chans : (k + 1) * chans, :] = dot(field, oh[k, 0:slots, :]).astype(BF)
+
+        unrolled(0, koff, inner)
         halo.wait()
         edge = hr[at, 0].astype(F32) * has_prev + hr[at, 1].astype(F32) * has_next
-        tab[:, slots : slots + LANE] = edge.astype(BF)
-        table = tab[...]
-
-        def step(k):
-            gath[pl.ds(pl.multiple_of(k * chans, 16), chans), :] = dot(table, oh[k]).astype(BF)
-
-        unrolled(0, koff, step)
+        edge = edge.astype(BF)
+
+        def outer(k):
+            part = dot(edge, oh[k, slots : slots + LANE, :]).astype(BF)
+            gath[k * chans : (k + 1) * chans, :] += part
+
+        unrolled(0, koff, outer)
         rs_send[at] = dot(wt[...], gath[...])
         summing.start()
         own = rs_send[at, pl.ds(pl.multiple_of(x * chans, 16), chans), :]
@@ -545,10 +546,10 @@
         return own
 
     lend(voxels, halo1, 0)
-    conv1 = convolve(halo1, 0, gath1, wt1, sum1)
+    conv1 = convolve(voxels, halo1, 0, gath1, wt1, sum1)
     hidden = (conv1 * jax.nn.sigmoid(conv1) * keep1).astype(BF)
     lend(hidden, halo2, 1)
-    conv2 = convolve(halo2, 1, gath2, wt2, sum2)
+    conv2 = convolve(hidden, halo2, 1, gath2, wt2, sum2)
     summed = voxels.astype(F32) + keep2 * conv2
     grad_pre = cot[...].astype(F32) * slope_silu(summed)
     mine = pl.ds(pl.multiple_of(x * chans, 16), chans)
@@ -568,22 +569,23 @@
                 pushed[3 * j + i, chans : 2 * chans, :] = low[part]
 
         unrolled(0, koff // 3, ahead)
-        ret[...] = jnp.zeros_like(ret)
-
-        def step(k):
-            part = dot_nt(pushed[9 * k], oh[9 * k])
-            for i in range(9 * k + 1, 9 * k + 9):
-                part = part + dot_nt(pushed[i], oh[i])
-            ret[...] += part
-
-        unrolled(0, koff // 9, step)
-        border = ret[0:chans, slots : slots + LANE] + ret[chans : 2 * chans, slots : slots + LANE]
+        both = returned(slots, slots + LANE)
+        border = both[0:chans] + both[chans : 2 * chans]
         fs[at, 0] = border
         fs[at, 1] = border
         fold.start()
 
+    def returned(low, high):
+        part = dot_nt(pushed[0], oh[0, low:high, :])
+        for k in range(1, koff):
+            part = part + dot_nt(pushed[k], oh[k, low:high, :])
+        return part
+
+    def own_columns():
+        ret[...] = returned(0, slots)
+
     def folded(fold, at):
-        own = ret[0:chans, 0:slots] + ret[chans : 2 * chans, 0:slots]
+        own = ret[0:chans, :] + ret[chans : 2 * chans, :]
         fold.wait()
         for part in split(fr[at, 0] * has_prev):
             own = own + dot_nt(part, lend_prev)
@@ -593,33 +595,37 @@
 
     share2.wait()
     push(w2, full_g.at[0], fold2, 0)
-    total2.compute(gath2, full_g.at[0])
+    own_columns()
+    total2.give(gath2, full_g.at[0])
     grad_hidden = folded(fold2, 0)
     full_g[1, mine, :] = (grad_hidden * keep1 * slope_silu(conv1)).astype(BF)
     share1.start()
+    total2.keep(gath2, full_g.at[0])
     total2.to_first()
     share1.wait()
-    total1.compute(gath1, full_g.at[1])
+    total1.give(gath1, full_g.at[1])
     push(w1, full_g.at[1], fold1, 1)
+    own_columns()
+    total1.keep(gath1, full_g.at[1])
     grad_voxels = (grad_pre + folded(fold1, 1)).astype(BF)
     wide = jnp.concatenate([grad_voxels, jnp.zeros((LANE - chans, slots), BF)], axis=0)
     bb_send[...] = dot_nt(em[...], wide).astype(BF)
     back_b.start()
     own_rows(bb_send, bb_recv, q, qa)
     total1.to_first()
+    total2.to_second()
     back_b.wait()
     perm_back = onehot(pc == (pr % qs) * qa + ((pr // qs) % 2) * ys + pr // ya)
     ba_send[...] = dot(perm_back, bb_recv[...]).astype(BF)
     back_a.start()
     own_rows(ba_send, ba_recv, y, ya)
-    total2.to_second()
+    total2.to_third()
+    total1.to_second()
     back_a.wait()
     gf = dot(ba_recv[...].astype(F32).T.astype(BF), pm[...])
     gf_ref[...] = gf[0:chans, :].astype(BF)
-    total1.to_second()
-    total2.to_third()
+    total2.to_fourth()
     total1.to_third()
-    total2.to_fourth()
     total1.to_fourth()
     total2.to_last()
     total1.to_last()
@@ -676,11 +682,10 @@
         vm((koff, table, slots), BF),
         vm((outs, padded), BF),
         vm((outs, padded), BF),
-        vm((chans, table), BF),
         vm((padded, slots), BF),
         vm((padded, slots), BF),
         vm((koff, 2 * chans, slots), BF),
-        vm((2 * chans, table), F32),
+        vm((2 * chans, slots), F32),
         vm((prows, scan), BF),
         vm((prows, slots), BF),
         vm((prows, prows), BF),

time: 109 us -> 104 us (0.954)
  Pallas kernels: 108 us -> 104 us
    pallas_call x1, Pallas kernels: 105 us -> 101 us  [local(): pl.pallas_call(functools.partial(kernel, dims), out_shape=(shape((chans,...]
where the time goes in v3:
time: 104 us
  Pallas kernels  104 us (100%)
    pallas_call x1, Pallas kernels, local(): pl.pallas_call(functools.partial(kernel, dims), out_shape=(shape((chans,...  101 us
    pallas_call x1, Pallas kernels, local(): pl.pallas_call(store, out_shape=(shape((chans, slots), BF), shape((chans,...  2.75 us

profile of v3, /device:TPU:1, one launch (start us, length us, event | category | flops | bytes accessed | tf_op | source)
XLA Modules:
  0.0 104.3 jit_solution(5362534935211270915)
XLA Ops:
  0.6 100.9 %block.1 = (bf16[64,256]{1,0:T(8,128)(2,1)}, bf16[64,128]{1,0:T(8,128)(2,1)}, bf16[1792,256]{1,0:T(8,128)(2,1)}, bf16[1792,256]{1,0:T(8,128)(2,1)}) custom-call(bf16[64,128]{1,0:T(8,128)(2,1)} %feat.1, s32[1,128]{1,0:T(1,128)} %bitcast.7, s32[2,32]{1,0:T(2,128)} %lists.1, s32[27,256]{1,0:T(8,128)} %kmap.1, s32[64,256]{1,0:T(8,128)} %drop1.1, ...), custom_call_target="tpu_custom_call" | custom-call | tf_op jit(solution)/shard_map/block/pallas_call | solution.py:718
  101.5 2.7 %store.1 = (bf16[64,256]{1,0:T(8,128)(2,1)}, bf16[64,128]{1,0:T(8,128)(2,1)}, bf16[1728,256]{1,0:T(8,128)(2,1)}, bf16[1728,256]{1,0:T(8,128)(2,1)}) custom-call(bf16[64,256]{1,0:T(8,128)(2,1)} %get-tuple-element.12.refs_0_, bf16[64,128]{1,0:T(8,128)(2,1)} %get-tuple-element.13.refs_1_, bf16[1792,256]{1,0:T(8,128)(2,1)} %get-tuple-element.14.refs_2_, ...), custom_call_target="tpu_custom_call" | custom-call | tf_op jit(solution)/shard_map/store/pallas_call | solution.py:738

commit v4 on v3

--- a/solution.py
+++ b/solution.py
@@ -441,13 +441,12 @@
                 self.last[side].start_one(1)
 
         def to_last(self):
-            for side, swap in enumerate(self.fourth):
-
-                def forward(d, swap=swap, side=side):
-                    swap.wait_one(d)
-                    self.last[side].start_one(d + 1)
-
-                loop(1, swap.n, forward)
+            for i in range(max(ys, zs) - 1):
+                for side, swap in enumerate(self.fourth):
+                    if i < swap.n - 1:
+                        d = 1 + i // 2 if i % 2 == 0 else swap.n - 1 - i // 2
+                        swap.wait_one(d)
+                        self.last[side].start_one(d + 1)
 
         def finish(self):
             for swap in self.last:
@@ -605,28 +604,28 @@
     share1.wait()
     total1.give(gath1, full_g.at[1])
     push(w1, full_g.at[1], fold1, 1)
+    total1.keep(gath1, full_g.at[1])
+    total1.to_first()
     own_columns()
-    total1.keep(gath1, full_g.at[1])
+    total2.to_second()
     grad_voxels = (grad_pre + folded(fold1, 1)).astype(BF)
     wide = jnp.concatenate([grad_voxels, jnp.zeros((LANE - chans, slots), BF)], axis=0)
     bb_send[...] = dot_nt(em[...], wide).astype(BF)
     back_b.start()
     own_rows(bb_send, bb_recv, q, qa)
-    total1.to_first()
-    total2.to_second()
+    perm_back = onehot(pc == (pr % qs) * qa + ((pr // qs) % 2) * ys + pr // ya)
+    total1.to_second()
+    total2.to_third()
     back_b.wait()
-    perm_back = onehot(pc == (pr % qs) * qa + ((pr // qs) % 2) * ys + pr // ya)
     ba_send[...] = dot(perm_back, bb_recv[...]).astype(BF)
     back_a.start()
     own_rows(ba_send, ba_recv, y, ya)
-    total2.to_third()
-    total1.to_second()
+    total1.to_third()
+    total2.to_fourth()
+    total1.to_fourth()
     back_a.wait()
     gf = dot(ba_recv[...].astype(F32).T.astype(BF), pm[...])
     gf_ref[...] = gf[0:chans, :].astype(BF)
-    total2.to_fourth()
-    total1.to_third()
-    total1.to_fourth()
     total2.to_last()
     total1.to_last()
     total2.finish()

time: 104 us -> 101 us (0.971)
  Pallas kernels: 104 us -> 100 us
    pallas_call x1, Pallas kernels: 101 us -> 97.3 us  [local(): pl.pallas_call(functools.partial(kernel, dims), out_shape=(shape((chans,...]
where the time goes in v4:
time: 101 us
  Pallas kernels  100 us (99%)
    pallas_call x1, Pallas kernels, local(): pl.pallas_call(functools.partial(kernel, dims), out_shape=(shape((chans,...  97.3 us
    pallas_call x1, Pallas kernels, local(): pl.pallas_call(store, out_shape=(shape((chans, slots), BF), shape((chans,...  2.75 us

profile of v4, /device:TPU:1, one launch (start us, length us, event | category | flops | bytes accessed | tf_op | source)
XLA Modules:
  0.0 100.7 jit_solution(5325175092445769575)
XLA Ops:
  0.6 97.3 %block.1 = (bf16[64,256]{1,0:T(8,128)(2,1)}, bf16[64,128]{1,0:T(8,128)(2,1)}, bf16[1792,256]{1,0:T(8,128)(2,1)}, bf16[1792,256]{1,0:T(8,128)(2,1)}) custom-call(bf16[64,128]{1,0:T(8,128)(2,1)} %feat.1, s32[1,128]{1,0:T(1,128)} %bitcast.7, s32[2,32]{1,0:T(2,128)} %lists.1, s32[27,256]{1,0:T(8,128)} %kmap.1, s32[64,256]{1,0:T(8,128)} %drop1.1, ...), custom_call_target="tpu_custom_call" | custom-call | tf_op jit(solution)/shard_map/block/pallas_call | solution.py:717
  97.9 2.7 %store.1 = (bf16[64,256]{1,0:T(8,128)(2,1)}, bf16[64,128]{1,0:T(8,128)(2,1)}, bf16[1728,256]{1,0:T(8,128)(2,1)}, bf16[1728,256]{1,0:T(8,128)(2,1)}) custom-call(bf16[64,256]{1,0:T(8,128)(2,1)} %get-tuple-element.12.refs_0_, bf16[64,128]{1,0:T(8,128)(2,1)} %get-tuple-element.13.refs_1_, bf16[1792,256]{1,0:T(8,128)(2,1)} %get-tuple-element.14.refs_2_, ...), custom_call_target="tpu_custom_call" | custom-call | tf_op jit(solution)/shard_map/store/pallas_call | solution.py:737

commit v5 on v4

--- a/solution.py
+++ b/solution.py
@@ -83,7 +83,7 @@
         unrolled(1, self.n, self.wait_one)
 
     def done(self):
-        loop(1, self.n, lambda d: self._copy(d, self.src(d), self.dst(d)).wait_send())
+        unrolled(1, self.n, lambda d: self._copy(d, self.src(d), self.dst(d)).wait_send())
 
 
 def sizes(bricks, ys, koff, chans, outs):
@@ -106,13 +106,19 @@
     kmap,
     drop1,
     drop2,
-    w1,
-    w2,
+    w1_hbm,
+    w2_hbm,
     cot,
     out_ref,
     gf_ref,
+    wg1_hbm,
+    wg2_hbm,
+    w1,
+    w2,
     wg1_ref,
     wg2_ref,
+    rs_low,
+    io_sem,
     oh,
     wt1,
     wt2,
@@ -169,10 +175,21 @@
     to_ch = lambda d: (b, ring(chs, x, d))
     to_brick = lambda d: (lax.rem(b + 1 + (d - 1) * (bricks - 2), bricks), x)
 
+    fetches = [
+        pltpu.make_async_copy(source, target, io_sem.at[i])
+        for i, (source, target) in enumerate(((w1_hbm, w1), (w2_hbm, w2)))
+    ]
+    for fetch in fetches:
+        fetch.start()
+    results = [
+        pltpu.make_async_copy(source.at[pl.ds(0, rows)], target, io_sem.at[2 + i])
+        for i, (source, target) in enumerate(((wg1_ref, wg1_hbm), (wg2_ref, wg2_hbm)))
+    ]
+
     barrier = pltpu.get_barrier_semaphore()
     groups = ((to_y, ys), (to_q, qs), (to_ch, chs), (to_brick, 3))
     for peer, n in groups:
-        loop(
+        unrolled(
             1,
             n,
             lambda d, peer=peer: pl.semaphore_signal(
@@ -249,7 +266,7 @@
         return Swap(
             chs,
             to_ch,
-            lambda d: chunk_of(rs_send.at[at], ring(chs, x, d), chans),
+            lambda d: chunk_of(rs_low.at[at], ring(chs, x, d), chans),
             lambda d: rs_recv.at[at, d - 1],
             lambda d: rs_recv.at[at, d - 1],
             next(sem_at),
@@ -496,6 +513,8 @@
             tail = jnp.concatenate([tail, jnp.zeros((LANE - rows % LANE, tail.shape[1]), F32)], 0)
             target[:, blocks * LANE : (blocks + 1) * LANE] = tail.T.astype(BF)
 
+    for fetch in fetches:
+        fetch.wait()
     turn(w1, wt1)
     turn(w2, wt2)
     for gath in (gath1, gath2):
@@ -536,12 +555,14 @@
             gath[k * chans : (k + 1) * chans, :] += part
 
         unrolled(0, koff, outer)
-        rs_send[at] = dot(wt[...], gath[...])
+        partial = dot(wt[...], gath[...])
+        rs_low[at] = partial.astype(BF)
         summing.start()
+        rs_send[at] = partial
         own = rs_send[at, pl.ds(pl.multiple_of(x * chans, 16), chans), :]
         summing.wait()
         for d in range(chs - 1):
-            own = own + rs_recv[at, d]
+            own = own + rs_recv[at, d].astype(F32)
         return own
 
     lend(voxels, halo1, 0)
@@ -627,10 +648,6 @@
     gf = dot(ba_recv[...].astype(F32).T.astype(BF), pm[...])
     gf_ref[...] = gf[0:chans, :].astype(BF)
     total2.to_last()
-    total1.to_last()
-    total2.finish()
-    total1.finish()
-
     for swap in (
         swap_a,
         swap_b,
@@ -644,10 +661,21 @@
         sum2,
         share2,
         share1,
-        *total2.all,
-        *total1.all,
+        *total2.all[:-2],
+        *total1.all[:-4],
     ):
         swap.done()
+    total2.finish()
+    results[1].start()
+    total1.to_last()
+    for swap in (*total2.last, *total1.fourth):
+        swap.done()
+    total1.finish()
+    results[0].start()
+    for swap in total1.last:
+        swap.done()
+    for result in results:
+        result.wait()
 
 
 def store(*refs):
@@ -678,6 +706,12 @@
     vm = pltpu.VMEM
     table = slots + LANE
     scratch = [
+        vm((rows, outs), BF),
+        vm((rows, outs), BF),
+        vm((padded, outs), BF),
+        vm((padded, outs), BF),
+        vm((2, outs, slots), BF),
+        pltpu.SemaphoreType.DMA((4,)),
         vm((koff, table, slots), BF),
         vm((outs, padded), BF),
         vm((outs, padded), BF),
@@ -694,7 +728,7 @@
         vm((2, 2, chans, LANE), F32),
         vm((2, 2, chans, LANE), F32),
         vm((2, outs, slots), F32),
-        vm((2, chs - 1, chans, slots), F32),
+        vm((2, chs - 1, chans, slots), BF),
         vm((2, outs, slots), BF),
         vm((2, half, outs), F32),
         vm((2, half, outs), BF),
@@ -714,16 +748,17 @@
         scratch += [pltpu.SemaphoreType.DMA((n,))] * 2
     shape = jax.ShapeDtypeStruct
     spec = pl.BlockSpec(memory_space=pltpu.VMEM)
+    anywhere = pl.BlockSpec(memory_space=pl.ANY)
     results = pl.pallas_call(
         functools.partial(kernel, dims),
         out_shape=(
             shape((chans, slots), BF),
             shape((chans, scan), BF),
-            shape((padded, outs), BF),
-            shape((padded, outs), BF),
+            shape((rows, outs), BF),
+            shape((rows, outs), BF),
         ),
-        in_specs=[spec] * 9,
-        out_specs=(spec,) * 4,
+        in_specs=[spec] * 6 + [anywhere] * 2 + [spec],
+        out_specs=(spec, spec, anywhere, anywhere),
         scratch_shapes=scratch,
         compiler_params=pltpu.CompilerParams(
             collective_id=0, has_side_effects=True, vmem_limit_bytes=56 * 2**20
@@ -733,7 +768,6 @@
         features, owner_map.reshape(1, scan), send_lists, kernel_map, drop1, drop2,
         w1.reshape(rows, outs), w2.reshape(rows, outs), cotangent,
     )
-    anywhere = pl.BlockSpec(memory_space=pl.ANY)
     block_out, grad_features, wg1, wg2 = pl.pallas_call(
         store,
         out_shape=(

time: 101 us -> 98.8 us (0.978)
  Pallas kernels: 100 us -> 98 us
    pallas_call x1, Pallas kernels: 97.3 us -> 95.3 us  [local(): pl.pallas_call(functools.partial(kernel, dims), out_shape=(shape((chans,...]
where the time goes in v5:
time: 98.8 us; the launch traced here: 98.6 us
  Pallas kernels  98 us (99%)
    pallas_call x1, Pallas kernels, local(): pl.pallas_call(functools.partial(kernel, dims), out_shape=(shape((chans,...  95.3 us
    pallas_call x1, Pallas kernels, local(): pl.pallas_call(store, out_shape=(shape((chans, slots), BF), shape((chans,...  2.73 us

profile of v5, /device:TPU:1, one launch (start us, length us, event | category | flops | bytes accessed | tf_op | source)
XLA Modules:
  0.0 98.6 jit_solution(6632128371763089822)
XLA Ops:
  0.6 95.3 %block.1 = (bf16[64,256]{1,0:T(8,128)(2,1)}, bf16[64,128]{1,0:T(8,128)(2,1)}, bf16[1728,256]{1,0:T(8,128)(2,1)}, bf16[1728,256]{1,0:T(8,128)(2,1)}) custom-call(bf16[64,128]{1,0:T(8,128)(2,1)} %feat.1, s32[1,128]{1,0:T(1,128)} %bitcast.7, s32[2,32]{1,0:T(2,128)} %lists.1, s32[27,256]{1,0:T(8,128)} %kmap.1, s32[64,256]{1,0:T(8,128)} %drop1.1, ...), custom_call_target="tpu_custom_call" | custom-call | tf_op jit(solution)/shard_map/block/pallas_call | solution.py:752
  95.9 2.7 %store.1 = (bf16[64,256]{1,0:T(8,128)(2,1)}, bf16[64,128]{1,0:T(8,128)(2,1)}, bf16[1728,256]{1,0:T(8,128)(2,1)}, bf16[1728,256]{1,0:T(8,128)(2,1)}) custom-call(bf16[64,256]{1,0:T(8,128)(2,1)} %get-tuple-element.12.refs_0_, bf16[64,128]{1,0:T(8,128)(2,1)} %get-tuple-element.13.refs_1_, bf16[1728,256]{1,0:T(8,128)(2,1)} %get-tuple-element.14.refs_2_, ...), custom_call_target="tpu_custom_call" | custom-call | tf_op jit(solution)/shard_map/store/pallas_call | solution.py:771

commit v6 on v5

--- a/solution.py
+++ b/solution.py
@@ -100,21 +100,28 @@
 
 def kernel(
     dims,
+    *refs,
+):
+    sources, targets, held = refs[0:9], refs[9:13], refs[13:24]
+    feat, owner, lists, kmap, drop1, drop2, w1, w2, cot, out_ref, gf_ref = held
+    body(dims, sources, targets, feat, owner, lists, kmap, drop1, drop2, w1, w2, cot, out_ref, gf_ref, *refs[24:])
+
+
+def body(
+    dims,
+    sources,
+    targets,
     feat,
     owner,
     lists,
     kmap,
     drop1,
     drop2,
-    w1_hbm,
-    w2_hbm,
+    w1,
+    w2,
     cot,
     out_ref,
     gf_ref,
-    wg1_hbm,
-    wg2_hbm,
-    w1,
-    w2,
     wg1_ref,
     wg2_ref,
     rs_low,
@@ -175,17 +182,6 @@
     to_ch = lambda d: (b, ring(chs, x, d))
     to_brick = lambda d: (lax.rem(b + 1 + (d - 1) * (bricks - 2), bricks), x)
 
-    fetches = [
-        pltpu.make_async_copy(source, target, io_sem.at[i])
-        for i, (source, target) in enumerate(((w1_hbm, w1), (w2_hbm, w2)))
-    ]
-    for fetch in fetches:
-        fetch.start()
-    results = [
-        pltpu.make_async_copy(source.at[pl.ds(0, rows)], target, io_sem.at[2 + i])
-        for i, (source, target) in enumerate(((wg1_ref, wg1_hbm), (wg2_ref, wg2_hbm)))
-    ]
-
     barrier = pltpu.get_barrier_semaphore()
     groups = ((to_y, ys), (to_q, qs), (to_ch, chs), (to_brick, 3))
     for peer, n in groups:
@@ -196,6 +192,28 @@
                 barrier, inc=1, device_id=peer(d), device_id_type=MESH
             ),
         )
+
+    inputs = (feat, owner, lists, kmap, drop1, drop2, w1, w2, cot)
+    fetches = [
+        pltpu.make_async_copy(source, target, io_sem.at[i])
+        for i, (source, target) in enumerate(zip(sources, inputs))
+    ]
+    for fetch in fetches:
+        fetch.start()
+    lower, upper = pl.ds(0, half), pl.ds(half, rows - half)
+    leaving = (
+        (out_ref, targets[0]),
+        (gf_ref, targets[1]),
+        (wg2_ref.at[pl.ds(0, rows)], targets[3]),
+        (wg1_ref.at[lower], targets[2].at[lower]),
+        (wg1_ref.at[upper], targets[2].at[upper]),
+    )
+    results = [
+        pltpu.make_async_copy(source, target, io_sem.at[9 + i])
+        for i, (source, target) in enumerate(leaving)
+    ]
+    for fetch in fetches[0:2]:
+        fetch.wait()
 
     prows = 2 * bricks
     t_row = owner[...]
@@ -418,9 +436,9 @@
 
         def to_first(self):
             self.cores.wait()
-            both = wgf[self.at] + c_recv[self.at].astype(F32)
-            s1_src[self.at] = both.astype(BF)
-            for swap in self.first:
+            for swap, lanes in zip(self.first, (left, right)):
+                both = wgf[self.at, :, lanes] + c_recv[self.at, :, lanes].astype(F32)
+                s1_src[self.at, :, lanes] = both.astype(BF)
                 swap.start()
 
         def to_second(self):
@@ -491,6 +509,8 @@
         column = jnp.where(row < rim, row + slots, jnp.where(row >= slots + 2 * rim, -1, inner))
         oh[k] = onehot(iota(oh.shape[1:], 0) == column)
 
+    for fetch in fetches[2:4]:
+        fetch.wait()
     unrolled(0, koff // 3, build)
 
     swap_a.wait()
@@ -513,7 +533,7 @@
             tail = jnp.concatenate([tail, jnp.zeros((LANE - rows % LANE, tail.shape[1]), F32)], 0)
             target[:, blocks * LANE : (blocks + 1) * LANE] = tail.T.astype(BF)
 
-    for fetch in fetches:
+    for fetch in fetches[4:9]:
         fetch.wait()
     turn(w1, wt1)
     turn(w2, wt2)
@@ -576,6 +596,7 @@
     full_g[0, mine, :] = (grad_pre * keep2).astype(BF)
     share2.start()
     out_ref[...] = (summed * jax.nn.sigmoid(summed)).astype(BF)
+    results[0].start()
 
     def push(weight, grads, fold, at):
         g = grads[...]
@@ -647,6 +668,7 @@
     back_a.wait()
     gf = dot(ba_recv[...].astype(F32).T.astype(BF), pm[...])
     gf_ref[...] = gf[0:chans, :].astype(BF)
+    results[1].start()
     total2.to_last()
     for swap in (
         swap_a,
@@ -666,12 +688,29 @@
     ):
         swap.done()
     total2.finish()
-    results[1].start()
+    results[2].start()
     total1.to_last()
+
+    @pl.when(core == 0)
+    def _():
+        results[3].start()
+
+    @pl.when(core == 1)
+    def _():
+        results[4].start()
+
     for swap in (*total2.last, *total1.fourth):
         swap.done()
     total1.finish()
-    results[0].start()
+
+    @pl.when(core == 1)
+    def _():
+        results[3].start()
+
+    @pl.when(core == 0)
+    def _():
+        results[4].start()
+
     for swap in total1.last:
         swap.done()
     for result in results:
@@ -706,12 +745,21 @@
     vm = pltpu.VMEM
     table = slots + LANE
     scratch = [
+        vm((chans, scan), BF),
+        vm((1, scan), I32),
+        vm(send_lists.shape, I32),
+        vm((koff, slots), I32),
+        vm((chans, slots), I32),
+        vm((chans, slots), I32),
         vm((rows, outs), BF),
         vm((rows, outs), BF),
+        vm((chans, slots), BF),
+        vm((chans, slots), BF),
+        vm((chans, scan), BF),
         vm((padded, outs), BF),
         vm((padded, outs), BF),
         vm((2, outs, slots), BF),
-        pltpu.SemaphoreType.DMA((4,)),
+        pltpu.SemaphoreType.DMA((14,)),
         vm((koff, table, slots), BF),
         vm((outs, padded), BF),
         vm((outs, padded), BF),
@@ -757,8 +805,8 @@
             shape((rows, outs), BF),
             shape((rows, outs), BF),
         ),
-        in_specs=[spec] * 6 + [anywhere] * 2 + [spec],
-        out_specs=(spec, spec, anywhere, anywhere),
+        in_specs=[anywhere] * 9,
+        out_specs=(anywhere,) * 4,
         scratch_shapes=scratch,
         compiler_params=pltpu.CompilerParams(
             collective_id=0, has_side_effects=True, vmem_limit_bytes=56 * 2**20

time: 98.8 us -> 97.6 us (0.988)
  Pallas kernels: 98 us -> 96.8 us
    pallas_call x1, Pallas kernels: 95.3 us -> 94.1 us  [local(): pl.pallas_call(functools.partial(kernel, dims), out_shape=(shape((chans,...]
where the time goes in v6:
time: 97.6 us; the launch traced here: 97.5 us
  Pallas kernels  96.8 us (99%)
    pallas_call x1, Pallas kernels, local(): pl.pallas_call(functools.partial(kernel, dims), out_shape=(shape((chans,...  94.1 us
    pallas_call x1, Pallas kernels, local(): pl.pallas_call(store, out_shape=(shape((chans, slots), BF), shape((chans,...  2.73 us

profile of v6, /device:TPU:1, one launch (start us, length us, event | category | flops | bytes accessed | tf_op | source)
XLA Modules:
  0.0 97.5 jit_solution(1553173979936709573)
XLA Ops:
  0.6 94.1 %block.1 = (bf16[64,256]{1,0:T(8,128)(2,1)}, bf16[64,128]{1,0:T(8,128)(2,1)}, bf16[1728,256]{1,0:T(8,128)(2,1)}, bf16[1728,256]{1,0:T(8,128)(2,1)}) custom-call(bf16[64,128]{1,0:T(8,128)(2,1)} %refs_0_.1, s32[1,128]{1,0:T(1,128)} %bitcast.7, s32[2,32]{1,0:T(2,128)} %refs_2_.1, s32[27,256]{1,0:T(8,128)} %refs_3_.1, s32[64,256]{1,0:T(8,128)} %refs_4_.1, ...), custom_call_target="tpu_custom_call" | custom-call | tf_op jit(solution)/shard_map/block/pallas_call | solution.py:800
  94.8 2.7 %store.1 = (bf16[64,256]{1,0:T(8,128)(2,1)}, bf16[64,128]{1,0:T(8,128)(2,1)}, bf16[1728,256]{1,0:T(8,128)(2,1)}, bf16[1728,256]{1,0:T(8,128)(2,1)}) custom-call(bf16[64,256]{1,0:T(8,128)(2,1)} %get-tuple-element.12.refs_0_, bf16[64,128]{1,0:T(8,128)(2,1)} %get-tuple-element.13.refs_1_, bf16[1728,256]{1,0:T(8,128)(2,1)} %get-tuple-element.14.refs_2_, ...), custom_call_target="tpu_custom_call" | custom-call | tf_op jit(solution)/shard_map/store/pallas_call | solution.py:819

commit v7 on v6

--- a/solution.py
+++ b/solution.py
@@ -316,11 +316,11 @@
         def __init__(self, at, ref):
             self.at, self.ref = at, ref
             self.cores = Swap(
-                2,
-                to_core,
-                lambda d: wgb.at[at],
-                lambda d: c_recv.at[at],
-                lambda d: c_recv.at[at],
+                3,
+                lambda d: to_core(1),
+                lambda d: wgb.at[at, pl.ds((d - 1) * (half // 2), half // 2)],
+                lambda d: c_recv.at[at, pl.ds((d - 1) * (half // 2), half // 2)],
+                lambda d: c_recv.at[at, pl.ds((d - 1) * (half // 2), half // 2)],
                 next(sem_at),
             )
             src = s1_src.at[at]
@@ -426,9 +426,9 @@
                 )
 
         def give(self, gath, grads):
-            for span, part in self.compute(gath, grads, 1 - core):
+            for i, (span, part) in enumerate(self.compute(gath, grads, 1 - core)):
                 wgb[self.at, span, :] = part.astype(BF)
-            self.cores.start()
+                self.cores.start_one(i + 1)
 
         def keep(self, gath, grads):
             for span, part in self.compute(gath, grads, core):
@@ -790,7 +790,7 @@
         vm((2, 2, second, LANE), BF),
         vm((2, 2, max(ys, zs) * second, LANE), BF),
     ]
-    weight_sums = [1, ys - 1, zs - 1, zs - 1, ys - 1, zs - 1, ys - 1, ys - 1, zs - 1, ys, zs]
+    weight_sums = [2, ys - 1, zs - 1, zs - 1, ys - 1, zs - 1, ys - 1, ys - 1, zs - 1, ys, zs]
     copies = [ys - 1, qs - 1, qs - 1, ys - 1, 2, 2, 2, 2] + [chs - 1] * 4 + weight_sums * 2
     for n in copies:
         scratch += [pltpu.SemaphoreType.DMA((n,))] * 2

time: 97.6 us -> 96.2 us (0.986)
  Pallas kernels: 96.8 us -> 95.4 us
    pallas_call x1, Pallas kernels: 94.1 us -> 92.7 us  [local(): pl.pallas_call(functools.partial(kernel, dims), out_shape=(shape((chans,...]
where the time goes in v7:
time: 96.2 us; the launch traced here: 96 us
  Pallas kernels  95.4 us (99%)
    pallas_call x1, Pallas kernels, local(): pl.pallas_call(functools.partial(kernel, dims), out_shape=(shape((chans,...  92.7 us
    pallas_call x1, Pallas kernels, local(): pl.pallas_call(store, out_shape=(shape((chans, slots), BF), shape((chans,...  2.73 us

profile of v7, /device:TPU:1, one launch (start us, length us, event | category | flops | bytes accessed | tf_op | source)
XLA Modules:
  0.0 96.0 jit_solution(5058691481958266496)
XLA Ops:
  0.6 92.7 %block.1 = (bf16[64,256]{1,0:T(8,128)(2,1)}, bf16[64,128]{1,0:T(8,128)(2,1)}, bf16[1728,256]{1,0:T(8,128)(2,1)}, bf16[1728,256]{1,0:T(8,128)(2,1)}) custom-call(bf16[64,128]{1,0:T(8,128)(2,1)} %refs_0_.1, s32[1,128]{1,0:T(1,128)} %bitcast.7, s32[2,32]{1,0:T(2,128)} %refs_2_.1, s32[27,256]{1,0:T(8,128)} %refs_3_.1, s32[64,256]{1,0:T(8,128)} %refs_4_.1, ...), custom_call_target="tpu_custom_call" | custom-call | tf_op jit(solution)/shard_map/block/pallas_call | solution.py:800
  93.3 2.7 %store.1 = (bf16[64,256]{1,0:T(8,128)(2,1)}, bf16[64,128]{1,0:T(8,128)(2,1)}, bf16[1728,256]{1,0:T(8,128)(2,1)}, bf16[1728,256]{1,0:T(8,128)(2,1)}) custom-call(bf16[64,256]{1,0:T(8,128)(2,1)} %get-tuple-element.12.refs_0_, bf16[64,128]{1,0:T(8,128)(2,1)} %get-tuple-element.13.refs_1_, bf16[1728,256]{1,0:T(8,128)(2,1)} %get-tuple-element.14.refs_2_, ...), custom_call_target="tpu_custom_call" | custom-call | tf_op jit(solution)/shard_map/store/pallas_call | solution.py:819
